TPU v7x, 32 devices: a whole 2x2x4 slice. The times are simulated.
32 devices in a mesh: seq: 16 (over z, y, core), frame: 2 (over x).
Axes of the slice: x: 2, y: 2, z: 4, core: 2. Of those that a mesh axis runs over, the one named last changes fastest.
Arguments:
- tokens: bfloat16 [2, 32, 32, 512], P('frame', 'seq'), may hold values from -6 to 6
- row_select: bfloat16 [2, 32, 32, 64], P('frame', 'seq'), may hold values from -2 to 2
- row_decay: float32 [2, 8, 32, 32], P('frame', None, 'seq'), may hold values from -1.5 to 0, as said below
- row_gain: float32 [512], replicated, may hold values from 0.25 to 1.75
- row_skip: float32 [8], replicated, may hold values from 0.5 to 1.5
- row_in: bfloat16 [512, 512], replicated, may hold values from -0.25 to 0.25
- row_out: bfloat16 [512, 512], replicated, may hold values from -0.25 to 0.25
- col_select: bfloat16 [2, 32, 32, 64], P('frame', 'seq'), may hold values from -2 to 2
- col_decay: float32 [2, 8, 32, 32], P('frame', None, 'seq'), may hold values from -1.5 to 0, as said below
- col_gain: float32 [512], replicated, may hold values from 0.25 to 1.75
- col_skip: float32 [8], replicated, may hold values from 0.5 to 1.5
- col_in: bfloat16 [512, 512], replicated, may hold values from -0.25 to 0.25
- col_out: bfloat16 [512, 512], replicated, may hold values from -0.25 to 0.25
- cotangent: bfloat16 [2, 32, 32, 512], P('frame', 'seq'), may hold values from -6 to 6
Outputs:
- mixed: bfloat16 [2, 32, 32, 512], P('frame', 'seq')
- grad_tokens: bfloat16 [2, 32, 32, 512], P('frame', 'seq')
Inputs may be any that keep to these rules, and one draw needn't show every extreme that they name: `row_decay`: every entry is below zero. `col_decay`: every entry is below zero.
All inputs are finite; a program needn't handle non-finite values.
Results may differ from a plain program's by a relative error of at most 0.013.
Values may be sent and summed in bfloat16 or wider, within the bound.
A program may use at most 128 MiB of HBM per device.

v0:
```python
from functools import partial

import jax
import jax.numpy as jnp
from jax import lax
from jax.sharding import PartitionSpec as P

EPSILON = 1e-05
PRECISE = lax.Precision.HIGHEST


def entering_2(shard, axis, combine, identity, reverse):
    peers, mine = (lax.axis_size(axis), lax.axis_index(axis))
    everything = jax.tree.map(lambda part: lax.all_gather(part, axis), shard)
    start = jax.tree.map(
        lambda part, zero: jnp.broadcast_to(jnp.asarray(zero, part.dtype), part.shape),
        shard,
        identity,
    )

    def lap(k, before):
        at = peers - 1 - k if reverse else k
        reached = at > mine if reverse else at < mine
        new = combine(before, jax.tree.map(lambda part: part[at], everything))
        return jax.tree.map(lambda a, b: jnp.where(reached, a, b), new, before)

    return lax.fori_loop(0, peers, lap, start)


def carried_in(shard, axis, join, neutral, backward):
    count = lax.axis_size(axis)
    place = lax.axis_index(axis)
    ahead = count - 1 - place if backward else place
    gathered = jax.tree.map(
        lambda a, kind: lax.all_gather(a.astype(kind), axis),
        shard,
        jax.tree.map(lambda a: jnp.bfloat16 if a.dtype == jnp.float32 else a.dtype, shard),
    )
    state = jax.tree.map(lambda a, e: jnp.zeros_like(a) + jnp.asarray(e, a.dtype), shard, neutral)

    def one(lap, state):
        source = count - 1 - lap if backward else lap
        return join(
            state,
            jax.tree.map(
                lambda a, own: lax.dynamic_index_in_dim(a, source, 0, False).astype(own.dtype),
                gathered,
                shard,
            ),
        )

    return lax.fori_loop(0, ahead, one, state)


def norm_rows(values, norm_gain):
    floats = values.astype(jnp.float32)
    factor = lax.rsqrt(jnp.mean(floats * floats, axis=-1, keepdims=True) + EPSILON)
    return (floats * factor * norm_gain).astype(jnp.bfloat16)


def block_terms(select_block, decay_block):
    extent = decay_block.shape[1]
    half_width = select_block.shape[1] // 2
    summed = jnp.cumsum(decay_block, axis=1)
    inward = jnp.sqrt(-jnp.expm1(2.0 * decay_block))
    target = lax.broadcasted_iota(jnp.int32, (extent, extent), 0)
    source = lax.broadcasted_iota(jnp.int32, (extent, extent), 1)
    causal = (target >= source).astype(jnp.float32)
    gap_sums = jnp.minimum(summed[:, :, None] - summed[:, None, :], 0.0)
    affinity = lax.dot_general(
        select_block[:, half_width:],
        select_block[:, :half_width],
        (((1,), (1,)), ((), ())),
        preferred_element_type=jnp.float32,
    )
    mixing = (jnp.exp(gap_sums) * causal * affinity[None] * inward[:, None, :]).astype(jnp.bfloat16)
    opening = jnp.exp(summed)
    ending = jnp.exp(summed[:, -1:] - summed) * inward
    return (mixing, opening, ending, jnp.exp(summed[:, -1]))


def forward_block(memory, block_piece, skip_gain):
    values, select_block, decay_block = block_piece
    half_width = select_block.shape[1] // 2
    mixing, opening, ending, through = block_terms(select_block, decay_block)
    floats = values.astype(jnp.float32)
    readout = select_block[:, half_width:].astype(jnp.float32)
    within = jnp.einsum("hts,shp->thp", mixing, values, preferred_element_type=jnp.float32)
    carried = jnp.einsum("tn,hpn->thp", readout, memory, precision=PRECISE) * opening.T[:, :, None]
    output = within + carried + skip_gain[None, :, None] * floats
    weighted = (floats * ending.T[:, :, None]).astype(jnp.bfloat16)
    memory = through[:, None, None] * memory + jnp.einsum(
        "shp,sn->hpn", weighted, select_block[:, :half_width], preferred_element_type=jnp.float32
    )
    return (memory, output)


def backward_block(memory, block_piece, skip_gain):
    values, select_block, decay_block = block_piece
    half_width = select_block.shape[1] // 2
    mixing, opening, ending, through = block_terms(select_block, decay_block)
    floats = values.astype(jnp.float32)
    writein = select_block[:, :half_width].astype(jnp.float32)
    within = jnp.einsum("hts,thp->shp", mixing, values, preferred_element_type=jnp.float32)
    carried = jnp.einsum("sn,hpn->shp", writein, memory, precision=PRECISE) * ending.T[:, :, None]
    output = within + carried + skip_gain[None, :, None] * floats
    weighted = (floats * opening.T[:, :, None]).astype(jnp.bfloat16)
    memory = through[:, None, None] * memory + jnp.einsum(
        "thp,tn->hpn", weighted, select_block[:, half_width:], preferred_element_type=jnp.float32
    )
    return (memory, output)


def local_pass(values, select, decay, skip_gain, backward):
    series_extent, model_width = values.shape
    head_count = decay.shape[0]
    half_width = select.shape[1] // 2
    block_size = min(512, series_extent)
    block_count = series_extent // block_size
    pieces = (
        values.reshape(block_count, block_size, head_count, model_width // head_count),
        select.reshape(block_count, block_size, select.shape[1]),
        decay.reshape(head_count, block_count, block_size).transpose(1, 0, 2),
    )
    zero_state = jnp.zeros((head_count, model_width // head_count, half_width), jnp.float32)
    advance = partial(backward_block if backward else forward_block, skip_gain=skip_gain)
    last_state, results = lax.scan(advance, zero_state, pieces, reverse=backward)
    summed = jnp.cumsum(decay, axis=1)
    return (results.reshape(series_extent, head_count, -1), last_state, summed)


def combine(earlier, later):
    return (earlier[0] * later[0], later[0][:, None, None] * earlier[1] + later[1])


def add_logs(earlier, later):
    return earlier + later


def carry_chain(device_pair, spent, backward):
    identity = (jnp.ones_like(device_pair[0]), jnp.zeros_like(device_pair[1]))
    before = entering_2(device_pair, "seq", combine, identity, backward)
    outside = entering_2(spent, "seq", add_logs, jnp.zeros_like(spent), not backward)
    decayed = jnp.exp(outside)[:, None, None] * device_pair[1]
    group_state, group_spent = lax.psum((decayed, spent), "seq")
    group = (jnp.exp(group_spent), group_state)
    earlier = carried_in(group, "frame", combine, identity, backward)
    return combine(earlier, before)[1]


def forward_start(inputs, select, decay, norm_gain, skip_gain, weight_in):
    normed = norm_rows(inputs, norm_gain)
    projected = jnp.dot(normed, weight_in, preferred_element_type=jnp.float32).astype(jnp.bfloat16)
    return local_pass(projected, select, decay, skip_gain, False)


def forward_finish(inputs, select, results, summed, entering, weight_out):
    series_extent, model_width = inputs.shape
    half_width = select.shape[1] // 2
    readout = select[:, half_width:].astype(jnp.float32)
    carried = (
        jnp.einsum("tn,hpn->thp", readout, entering, precision=PRECISE)
        * jnp.exp(summed).T[:, :, None]
    )
    scanned = (results + carried).reshape(series_extent, model_width).astype(jnp.bfloat16)
    total = inputs.astype(jnp.float32) + jnp.dot(
        scanned, weight_out, preferred_element_type=jnp.float32
    )
    return total.astype(jnp.bfloat16)


def backward_start(incoming, select, decay, skip_gain, weight_out):
    pulled = lax.dot_general(
        incoming, weight_out, (((1,), (1,)), ((), ())), preferred_element_type=jnp.float32
    ).astype(jnp.bfloat16)
    return local_pass(pulled, select, decay, skip_gain, True)


def backward_finish(
    inputs, incoming, select, decay, results, summed, entering, norm_gain, weight_in
):
    series_extent, model_width = inputs.shape
    half_width = select.shape[1] // 2
    inward = jnp.sqrt(-jnp.expm1(2.0 * decay))
    ending = jnp.exp(summed[:, -1:] - summed) * inward
    writein = select[:, :half_width].astype(jnp.float32)
    carried = jnp.einsum("sn,hpn->shp", writein, entering, precision=PRECISE) * ending.T[:, :, None]
    scanned = (results + carried).reshape(series_extent, model_width).astype(jnp.bfloat16)
    returned = lax.dot_general(
        scanned, weight_in, (((1,), (1,)), ((), ())), preferred_element_type=jnp.float32
    )
    floats = inputs.astype(jnp.float32)
    factor = lax.rsqrt(jnp.mean(floats * floats, axis=-1, keepdims=True) + EPSILON)
    scaled = norm_gain * returned
    result = (
        incoming.astype(jnp.float32)
        + factor * scaled
        - floats * factor**3 * jnp.mean(scaled * floats, axis=-1, keepdims=True)
    )
    return result.astype(jnp.bfloat16)


def mixer_forward(inputs, select, decay, norm_gain, skip_gain, weight_in, weight_out):
    results, last_state, summed = forward_start(
        inputs, select, decay, norm_gain, skip_gain, weight_in
    )
    spent = summed[:, -1]
    entering = carry_chain((jnp.exp(spent), last_state), spent, False)
    return forward_finish(inputs, select, results, summed, entering, weight_out)


def mixer_backward(inputs, incoming, select, decay, norm_gain, skip_gain, weight_in, weight_out):
    results, last_state, summed = backward_start(incoming, select, decay, skip_gain, weight_out)
    spent = summed[:, -1]
    entering = carry_chain((jnp.exp(spent), last_state), spent, True)
    return backward_finish(
        inputs, incoming, select, decay, results, summed, entering, norm_gain, weight_in
    )


def body(
    tokens,
    row_select,
    row_decay,
    row_gain,
    row_skip,
    row_in,
    row_out,
    col_select,
    col_decay,
    col_gain,
    col_skip,
    col_in,
    col_out,
    cotangent,
):
    model_width = tokens.shape[-1]
    head_count = row_decay.shape[1]
    doubled = row_select.shape[-1]
    row_share = row_decay.shape[2]
    col_share = col_decay.shape[2]
    seq_count = lax.axis_size("seq")
    row_inputs = tokens.reshape(-1, model_width)
    row_lam = row_decay.reshape(head_count, -1)
    col_lam = col_decay.reshape(head_count, -1)
    row_vectors = row_select.reshape(-1, doubled)
    col_vectors = col_select.reshape(-1, doubled)
    row_mixed = mixer_forward(row_inputs, row_vectors, row_lam, row_gain, row_skip, row_in, row_out)
    sending = row_mixed.reshape(row_share, seq_count, col_share, model_width).transpose(2, 1, 0, 3)
    arrived = lax.all_to_all(sending, "seq", split_axis=1, concat_axis=1, tiled=True)
    col_tokens = arrived.reshape(-1, model_width)
    incoming = cotangent.reshape(-1, model_width)
    mixed = mixer_forward(col_tokens, col_vectors, col_lam, col_gain, col_skip, col_in, col_out)
    col_grad = mixer_backward(
        col_tokens, incoming, col_vectors, col_lam, col_gain, col_skip, col_in, col_out
    )
    returning = col_grad.reshape(col_share, seq_count, row_share, model_width)
    landed = lax.all_to_all(returning, "seq", split_axis=1, concat_axis=1, tiled=True)
    row_grad = landed.transpose(2, 1, 0, 3).reshape(-1, model_width)
    grad_tokens = mixer_backward(
        row_inputs, row_grad, row_vectors, row_lam, row_gain, row_skip, row_in, row_out
    )
    return (mixed.reshape(cotangent.shape), grad_tokens.reshape(tokens.shape))


def solution(mesh):
    placed = (
        P("frame", "seq", None, None),
        P("frame", "seq", None, None),
        P("frame", None, "seq", None),
        P(),
        P(),
        P(),
        P(),
        P("frame", "seq", None, None),
        P("frame", None, "seq", None),
        P(),
        P(),
        P(),
        P(),
        P("frame", "seq", None, None),
    )
    return jax.shard_map(
        body,
        mesh=mesh,
        in_specs=placed,
        out_specs=(P("frame", "seq", None, None), P("frame", "seq", None, None)),
        check_vma=False,
    )
```

profile of v0, /device:TPU:0, one launch (start us, length us, event | category | flops | bytes accessed | tf_op | source)
XLA Modules:
  0.0 392.9 jit_solution(15823295367507647754)
XLA Ops:
  10.4 1.2 dynamic-slice
  12.7 34.9 %all-reduce.8 = (f32[128]{0:T(128)S(1)}, f32[128]{0:T(128)S(1)}) all-reduce(f32[128]{0:T(128)S(1)} %dynamic-update-slice.2, f32[128]{0:T(128)S(1)} %dynamic-update-slice.5), channel_id=4, replica_groups=mesh['seq'=16,'frame'=2] {'seq'}, use_global_device_ids=true, to_apply=%add.2 | all-reduce | flops 256 | bytes 2048
  48.4 1.4 convolution_convert_fusion.1
  49.9 1.7 broadcast_multiply_fusion.1
  52.5 0.9 fusion.52
  53.5 0.9 fusion.47
  60.9 62.3 %all-reduce.12 = (f32[128]{0:T(128)}, f32[8]{0:T(128)S(1)}, bf16[8,64,32]{1,2,0:T(8,128)(2,1)S(1)}, f32[128]{0:T(128)S(1)}, f32[8]{0:T(128)S(1)}, /*index=5*/bf16[8,64,32]{1,2,0:T(8,128)(2,1)S(1)}) all-reduce(f32[128]{0:T(128)S(1)} %dynamic-update-slice, f32[8]{0:T(128)S(1)} %get-tuple-element.1632, ...), channel_id=14, replica_groups=mesh['seq'=16,'frame'=2] {'seq'}, use_global_device_ids=true, to_apply=%add | all-reduce | flops 33040 | bytes 198784
  123.7 4.9 %all-reduce.9 = (bf16[16]{0:T(256)(128)(2,1)S(1)}, bf16[16]{0:T(256)(128)(2,1)S(1)}) all-reduce(bf16[16]{0:T(256)(128)(2,1)S(1)} %dynamic-update-slice.1, bf16[16]{0:T(256)(128)(2,1)S(1)} %dynamic-update-slice.4), channel_id=3, replica_groups=mesh['seq'=16,'frame'=2] {'frame'}, use_global_device_ids=true, to_apply=%add.1 | all-reduce | flops 32 | bytes 128
  128.7 4.9 %all-gather.9 = bf16[16,64,32]{1,2,0:T(8,128)(2,1)S(1)} all-gather(bf16[8,64,32]{1,2,0:T(8,128)(2,1)S(1)} %get-tuple-element.1761), channel_id=11, replica_groups=mesh['seq'=16,'frame'=2] {'frame'}, dimensions={0}, use_global_device_ids=true | all-gather | bytes 98304 | tf_op jit(solution)/shard_map/all_gather | solution.py:35
  134.5 4.9 %all-gather.3 = bf16[16,64,32]{1,2,0:T(8,128)(2,1)S(1)} all-gather(bf16[8,64,32]{1,2,0:T(8,128)(2,1)S(1)} %get-tuple-element.1758), channel_id=5, replica_groups=mesh['seq'=16,'frame'=2] {'frame'}, dimensions={0}, use_global_device_ids=true | all-gather | bytes 98304 | tf_op jit(solution)/shard_map/all_gather | solution.py:35
  143.6 1.1 convolution_bitcast_fusion.11
  144.7 1.6 fusion.13
  146.3 1.1 fusion.23
  147.4 19.4 %while.208 = (s32[]{:T(128)}, f32[8]{0:T(128)S(1)}, f32[8,64,32]{2,1,0:T(8,128)S(1)}, s32[]{:T(128)}, f32[16,8]{1,0:T(8,128)S(1)}, /*index=5*/f32[16,8,64,32]{2,...) while((s32[]{:T(128)}, f32[8]{0:T(128)S(1)}, f32[8,64,32]{2,1,0:T(8,128)S(1)}, ...), condition=%wide.region_21.22_spmd.clone, body=%wide.region_20.21_spmd.clone.sunk | while | flops 65568 | bytes 459089 | solution.py:27
  148.6 0.9 constant_dynamic-slice_fusion.22
  149.8 0.9 constant_dynamic-slice_fusion.22
  151.0 0.9 constant_dynamic-slice_fusion.22
  152.2 0.9 constant_dynamic-slice_fusion.22
  153.4 0.9 constant_dynamic-slice_fusion.22
  154.6 0.9 constant_dynamic-slice_fusion.22
  155.9 0.9 constant_dynamic-slice_fusion.22
  157.1 0.9 constant_dynamic-slice_fusion.22
  158.3 0.9 constant_dynamic-slice_fusion.22
  159.5 0.9 constant_dynamic-slice_fusion.22
  160.7 0.9 constant_dynamic-slice_fusion.22
  161.9 0.9 constant_dynamic-slice_fusion.22
  163.1 0.9 constant_dynamic-slice_fusion.22
  164.4 0.9 constant_dynamic-slice_fusion.22
  165.6 0.9 constant_dynamic-slice_fusion.22
  167.3 49.1 %while.204 = (s32[]{:T(128)}, f32[8]{0:T(128)}, f32[8,64,32]{2,1,0:T(8,128)S(1)}, s32[]{:T(128)}, f32[16,8]{1,0:T(8,128)}, /*index=5*/f32[16,8,64,32]{2,3,1,0:T(8,128)}, s32[]{:T(128)}, s32[]{:T(128)}) while((s32[]{:T(128)}, f32[8]{0:T(128)}, f32[8,64,32]{2,1,0:T(8,128)S(1)}, s32[]{:T(128)}, f32[16,8]{1,0:T(8,128)}, ...), condition=%wide.region_3.4_spmd.clone, body=%wide.region_2.3_spmd.clone.sunk | while | flops 65564 | bytes 459027 | solution.py:27
  167.3 1.3 broadcast_select_fusion.24
  170.4 1.3 broadcast_select_fusion.24
  173.5 1.3 broadcast_select_fusion.24
  176.5 1.3 broadcast_select_fusion.24
  179.6 1.3 broadcast_select_fusion.24
  182.6 1.3 broadcast_select_fusion.24
  185.7 1.3 broadcast_select_fusion.24
  188.8 1.3 broadcast_select_fusion.24
  191.8 1.3 broadcast_select_fusion.24
  194.9 1.3 broadcast_select_fusion.24
  198.0 1.3 broadcast_select_fusion.24
  201.1 1.3 broadcast_select_fusion.24
  204.1 1.3 broadcast_select_fusion.24
  207.2 1.3 broadcast_select_fusion.24
  210.3 1.3 broadcast_select_fusion.24
  213.3 1.3 broadcast_select_fusion.24
  216.4 1.4 fusion.24
  217.8 1.1 fusion.28
  219.6 3.5 all-to-all-start
  223.2 1.0 fusion.26
  224.2 5.8 %all-to-all-done = bf16[2,16,2,512]{3,0,2,1:T(2,128)(2,1)S(1)} async-done(((bf16[2,16,2,512]{3,0,2,1:T(2,128)(2,1)}), bf16[2,16,2,512]{3,0,2,1:T(2,128)(2,1)S(1)}, u32[]{:S(2)}, u32[]{:S(2)}) %all-to-all-start) | async-done | bytes 65568 | tf_op jit(solution)/shard_map/all_to_all | solution.py:250
  232.1 3.5 all-to-all-start.1
  237.2 1.0 fusion.18
  238.2 4.3 %all-to-all-done.1 = bf16[2,16,2,512]{3,0,2,1:T(2,128)(2,1)S(1)} async-done(((bf16[2,16,2,512]{3,0,2,1:T(2,128)(2,1)}), bf16[2,16,2,512]{3,0,2,1:T(2,128)(2,1)S(1)}, u32[]{:S(2)}, u32[]{:S(2)}) %all-to-all-start.1) | async-done | bytes 65568 | tf_op jit(solution)/shard_map/all_to_all | solution.py:258
  243.4 1.0 broadcast_multiply_fusion
  244.4 60.8 %all-reduce.13 = (bf16[8,64,32]{1,2,0:T(8,128)(2,1)S(1)}, bf16[8,64,32]{1,2,0:T(8,128)(2,1)S(1)}) all-reduce(f32[8,64,32]{1,2,0:T(8,128)S(1)} %get-tuple-element.1784, f32[8,64,32]{1,2,0:T(8,128)S(1)} %get-tuple-element.1788), channel_id=1, replica_groups=mesh['seq'=16,'frame'=2] {'seq'}, use_global_device_ids=true, to_apply=%region_17.18 | all-reduce | flops 32768 | bytes 196608 | tf_op jit(solution)/shard_map/psum | solution.py:145
  305.2 5.2 %all-gather.7 = bf16[16,64,32]{1,2,0:T(8,128)(2,1)S(1)} all-gather(bf16[8,64,32]{1,2,0:T(8,128)(2,1)S(1)} %get-tuple-element.1754), channel_id=9, replica_groups=mesh['seq'=16,'frame'=2] {'frame'}, dimensions={0}, use_global_device_ids=true | all-gather | bytes 98304 | tf_op jit(solution)/shard_map/all_gather | solution.py:35
  311.3 4.9 %all-gather.11 = bf16[16,64,32]{1,2,0:T(8,128)(2,1)S(1)} all-gather(bf16[8,64,32]{1,2,0:T(8,128)(2,1)S(1)} %get-tuple-element.1755), channel_id=13, replica_groups=mesh['seq'=16,'frame'=2] {'frame'}, dimensions={0}, use_global_device_ids=true | all-gather | bytes 98304 | tf_op jit(solution)/shard_map/all_gather | solution.py:35
  316.9 30.1 %while.206 = (s32[]{:T(128)}, f32[8]{0:T(128)S(1)}, f32[8,64,32]{2,1,0:T(8,128)S(1)}, s32[]{:T(128)}, f32[16,8]{1,0:T(8,128)}, /*index=5*/f32[16,8,64,32]{2,3,1,0:T(8,128)}, s32[]{:T(128)}, s32[]{:T(128)}) while((s32[]{:T(128)}, f32[8]{0:T(128)S(1)}, f32[8,64,32]{2,1,0:T(8,128)S(1)}, s32[]{:T(128)}, f32[16,8]{1,0:T(8,128)}, ...), condition=%wide.region_13.14_spmd.clone, body=%wide.region_12.13_spmd.clone.sunk | while | flops 65564 | bytes 459027 | solution.py:27
  319.5 0.9 constant_dynamic-slice_fusion.21
  321.4 0.9 constant_dynamic-slice_fusion.21
  347.0 1.3 fusion.25
  349.2 5.5 %all-gather.25.cloned.1.call-done = f32[128,64,32]{1,2,0:T(8,128)} async-done(((f32[8,64,32]{1,2,0:T(8,128)}), f32[128,64,32]{1,2,0:T(8,128)}) %all-gather.25.cloned.1.call-update) | async-done | bytes 1048592 | tf_op jit(solution)/shard_map/all_gather | solution.py:14
  354.7 30.1 %while.210 = (s32[]{:T(128)}, f32[8]{0:T(128)S(1)}, f32[8,64,32]{2,1,0:T(8,128)S(1)}, s32[]{:T(128)}, f32[16,8]{1,0:T(8,128)}, /*index=5*/f32[16,8,64,32]{2,3,1,...) while((s32[]{:T(128)}, f32[8]{0:T(128)S(1)}, f32[8,64,32]{2,1,0:T(8,128)S(1)}, s32[]{:T(128)}, ...), condition=%wide.region_29.30_spmd.clone, body=%wide.region_28.29_spmd.clone.sunk | while | flops 65568 | bytes 459089 | solution.py:27
  (521 shorter events, 117.5 us)
Async XLA Ops:
  7.2 223.4 %copy-start = (bf16[512,512]{1,0:T(8,128)(2,1)S(1)}, bf16[512,512]{1,0:T(8,128)(2,1)}, u32[]{:S(2)}) copy-start(bf16[512,512]{1,0:T(8,128)(2,1)} %param.49) | copy-start | bytes 1572868
  7.2 52.0 %copy-start.57 = (u32[32]{0:T(128)S(1)}, u32[32]{0:T(128)}, u32[]{:S(2)}) copy-start(u32[32]{0:T(128)} %constant.435) | copy-start | bytes 388
  7.2 49.2 %copy-start.5 = (bf16[1,2,32,64]{3,2,1,0:T(8,128)(2,1)S(1)}, bf16[1,2,32,64]{3,2,1,0:T(8,128)(2,1)}, u32[]{:S(2)}) copy-start(bf16[1,2,32,64]{3,2,1,0:T(8,128)(2,1)} %param.45) | copy-start | bytes 24580
  7.2 47.3 %copy-start.2 = (bf16[512,512]{1,0:T(8,128)(2,1)S(1)}, bf16[512,512]{1,0:T(8,128)(2,1)}, u32[]{:S(2)}) copy-start(bf16[512,512]{1,0:T(8,128)(2,1)} %param.43) | copy-start | bytes 1572868
  7.2 48.2 %copy-start.6 = (bf16[1,2,32,64]{3,2,1,0:T(8,128)(2,1)S(1)}, bf16[1,2,32,64]{3,2,1,0:T(8,128)(2,1)}, u32[]{:S(2)}) copy-start(bf16[1,2,32,64]{3,2,1,0:T(8,128)(2,1)} %param.39) | copy-start | bytes 24580
  7.2 140.1 %all-gather.23.cloned.1.call-start = ((), (), s32[]{:S(2)}) async-start(), calls=%async_computation.4 | async-start | bytes 2228224 | tf_op jit(solution)/shard_map/all_gather | solution.py:14
  8.4 134.9 %copy-start.21 = (f32[8,64]{1,0:T(8,128)}, f32[8,64]{1,0:T(8,128)S(1)}, u32[]{:S(2)}) copy-start(f32[8,64]{1,0:T(8,128)S(1)} %reduce_window_sum.28) | copy-start | bytes 6148
  9.2 45.3 %copy-start.10 = (f32[64,8]{0,1:T(8,128)}, f32[64,8]{0,1:T(8,128)S(1)}, u32[]{:S(2)}) copy-start(f32[64,8]{0,1:T(8,128)S(1)} %get-tuple-element.1776) | copy-start | bytes 6148
  9.2 135.5 %copy-start.15 = (f32[64,8]{0,1:T(8,128)}, f32[64,8]{0,1:T(8,128)S(1)}, u32[]{:S(2)}) copy-start(f32[64,8]{0,1:T(8,128)S(1)} %get-tuple-element.1774) | copy-start | bytes 6148
  9.2 42.5 %copy-start.45 = (f32[8]{0:T(128)}, f32[8]{0:T(128)S(1)}, u32[]{:S(2)}) copy-start(f32[8]{0:T(128)S(1)} %exponential_multiply_fusion) | copy-start | bytes 100
  10.2 133.4 %copy-start.19 = (f32[8,64]{1,0:T(8,128)}, f32[8,64]{1,0:T(8,128)S(1)}, u32[]{:S(2)}) copy-start(f32[8,64]{1,0:T(8,128)S(1)} %reduce_window_sum.27) | copy-start | bytes 6148
  51.6 115.2 %all-gather.19.cloned.1.call-start = ((), (), s32[]{:S(2)}) async-start(), calls=%async_computation.2 | async-start | bytes 2228224 | tf_op jit(solution)/shard_map/all_gather | solution.py:14
  53.5 80.1 %copy-start.43 = (f32[64]{0:T(128)}, f32[64]{0:T(128)S(1)}, u32[]{:S(2)}) copy-start(f32[64]{0:T(128)S(1)} %rsqrt.31) | copy-start | bytes 772
  54.8 78.8 %copy-start.47 = (f32[8]{0:T(128)}, f32[8]{0:T(128)S(1)}, u32[]{:S(2)}) copy-start(f32[8]{0:T(128)S(1)} %exponential_multiply_fusion.1) | copy-start | bytes 100
  55.4 78.2 %copy-start.13 = (f32[64,8]{0,1:T(8,128)}, f32[64,8]{0,1:T(8,128)S(1)}, u32[]{:S(2)}) copy-start(f32[64,8]{0,1:T(8,128)S(1)} %get-tuple-element.1777) | copy-start | bytes 6148
  55.4 90.9 %copy-start.17 = (f32[64,8]{0,1:T(8,128)}, f32[64,8]{0,1:T(8,128)S(1)}, u32[]{:S(2)}) copy-start(f32[64,8]{0,1:T(8,128)S(1)} %get-tuple-element.1779) | copy-start | bytes 6148
  134.0 0.5 copy-start.55
  139.5 0.6 copy-start.52
  139.5 1.3 copy-start.33
  139.5 2.5 copy-start.32
  139.5 3.8 copy-start.23
  139.5 3.8 copy-start.26
  139.5 3.7 copy-start.36
  139.5 4.0 %copy-start.38 = (f32[8,64]{1,0:T(8,128)S(1)}, f32[8,64]{1,0:T(8,128)}, u32[]{:S(2)}) copy-start(f32[8,64]{1,0:T(8,128)} %get-tuple-element.1778) | copy-start | bytes 6148
  139.6 4.0 %copy-start.53 = (bf16[2,8]{1,0:T(2,128)(2,1)}, bf16[2,8]{1,0:T(2,128)(2,1)S(1)}, u32[]{:S(2)}) copy-start(bf16[2,8]{1,0:T(2,128)(2,1)S(1)} %get-tuple-element.2495) | copy-start | bytes 100
  139.6 6.7 %copy-start.41 = (f32[8]{0:T(128)S(1)}, f32[8]{0:T(128)}, u32[]{:S(2)}) copy-start(f32[8]{0:T(128)} %param.42) | copy-start | bytes 100
  166.7 0.6 copy-start.28
  166.8 0.6 copy-start.31
  166.8 51.0 %copy-start.1 = (bf16[512,512]{1,0:T(8,128)(2,1)S(1)}, bf16[512,512]{1,0:T(8,128)(2,1)}, u32[]{:S(2)}) copy-start(bf16[512,512]{1,0:T(8,128)(2,1)} %param.44) | copy-start | bytes 1572868
  216.4 6.7 %copy-start.8 = (f32[64,8,64]{0,2,1:T(8,128)S(1)}, f32[64,8,64]{0,2,1:T(8,128)}, u32[]{:S(2)}) copy-start(f32[64,8,64]{0,2,1:T(8,128)} %fusion.13) | copy-start | bytes 393220
  217.8 12.8 %copy-start.34 = (f32[512]{0:T(512)S(1)}, f32[512]{0:T(512)}, u32[]{:S(2)}) copy-start(f32[512]{0:T(512)} %param.47) | copy-start | bytes 6148
  218.9 12.4 %copy-start.9 = (bf16[1,2,32,512]{3,2,1,0:T(8,128)(2,1)S(1)}, bf16[1,2,32,512]{3,2,1,0:T(8,128)(2,1)}, u32[]{:S(2)}) copy-start(bf16[1,2,32,512]{3,2,1,0:T(8,128)(2,1)} %param.51) | copy-start | bytes 196612
  219.6 10.4 %all-to-all-start = ((bf16[2,16,2,512]{3,0,2,1:T(2,128)(2,1)}), bf16[2,16,2,512]{3,0,2,1:T(2,128)(2,1)S(1)}, u32[]{:S(2)}, u32[]{:S(2)}) async-start(bf16[2,16,2,512]{3,0,2,1:T(2,128)(2,1)} %bitcast.251), calls=%async_computation | async-start | bytes 131072 | tf_op jit(solution)/shard_map/all_to_all | solution.py:250
  223.1 12.7 %copy-start.22 = (f32[8,64]{1,0:T(8,128)S(1)}, f32[8,64]{1,0:T(8,128)}, u32[]{:S(2)}) copy-start(f32[8,64]{1,0:T(8,128)} %copy-done.21) | copy-start | bytes 6148
  223.1 12.7 %copy-start.24 = (f32[64,64]{1,0:T(8,128)S(1)}, f32[64,64]{1,0:T(8,128)}, u32[]{:S(2)}) copy-start(f32[64,64]{1,0:T(8,128)} %fusion.67) | copy-start | bytes 49156
  223.2 12.7 %copy-start.27 = (f32[64,64]{1,0:T(8,128)S(1)}, f32[64,64]{1,0:T(8,128)}, u32[]{:S(2)}) copy-start(f32[64,64]{1,0:T(8,128)} %fusion.82) | copy-start | bytes 49156
  223.2 12.7 %copy-start.37 = (f32[8,64]{1,0:T(8,128)S(1)}, f32[8,64]{1,0:T(8,128)}, u32[]{:S(2)}) copy-start(f32[8,64]{1,0:T(8,128)} %get-tuple-element.1775) | copy-start | bytes 6148
  224.2 12.0 %copy-start.16 = (f32[64,8]{0,1:T(8,128)S(1)}, f32[64,8]{0,1:T(8,128)}, u32[]{:S(2)}) copy-start(f32[64,8]{0,1:T(8,128)} %copy-done.15) | copy-start | bytes 6148
  224.2 12.0 %copy-start.46 = (f32[8]{0:T(128)S(1)}, f32[8]{0:T(128)}, u32[]{:S(2)}) copy-start(f32[8]{0:T(128)} %copy-done.45) | copy-start | bytes 100
  224.2 12.0 %copy-start.51 = (f32[8]{0:T(128)S(1)}, f32[8]{0:T(128)}, u32[]{:S(2)}) copy-start(f32[8]{0:T(128)} %exp.131) | copy-start | bytes 100
  230.1 7.1 %copy-start.11 = (f32[64,8]{0,1:T(8,128)S(1)}, f32[64,8]{0,1:T(8,128)}, u32[]{:S(2)}) copy-start(f32[64,8]{0,1:T(8,128)} %copy-done.10) | copy-start | bytes 6148
  230.1 7.1 %copy-start.40 = (f32[8]{0:T(128)S(1)}, f32[8]{0:T(128)}, u32[]{:S(2)}) copy-start(f32[8]{0:T(128)} %param.48) | copy-start | bytes 100
  231.2 11.8 %copy-start.20 = (f32[8,64]{1,0:T(8,128)S(1)}, f32[8,64]{1,0:T(8,128)}, u32[]{:S(2)}) copy-start(f32[8,64]{1,0:T(8,128)} %copy-done.19) | copy-start | bytes 6148
  231.2 11.8 %copy-start.25 = (f32[64,64]{1,0:T(8,128)S(1)}, f32[64,64]{1,0:T(8,128)}, u32[]{:S(2)}) copy-start(f32[64,64]{1,0:T(8,128)} %fusion.91) | copy-start | bytes 49156
  231.2 11.8 %copy-start.39 = (f32[8,64]{1,0:T(8,128)S(1)}, f32[8,64]{1,0:T(8,128)}, u32[]{:S(2)}) copy-start(f32[8,64]{1,0:T(8,128)} %get-tuple-element.1778) | copy-start | bytes 6148
  231.3 12.1 %copy-start.7 = (bf16[1,2,32,64]{3,2,1,0:T(8,128)(2,1)S(1)}, bf16[1,2,32,64]{3,2,1,0:T(8,128)(2,1)}, u32[]{:S(2)}) copy-start(bf16[1,2,32,64]{3,2,1,0:T(8,128)(2,1)} %param.39) | copy-start | bytes 24580
  231.3 12.1 %copy-start.18 = (f32[64,8]{0,1:T(8,128)S(1)}, f32[64,8]{0,1:T(8,128)}, u32[]{:S(2)}) copy-start(f32[64,8]{0,1:T(8,128)} %copy-done.17) | copy-start | bytes 6148
  231.3 12.1 %copy-start.48 = (f32[8]{0:T(128)S(1)}, f32[8]{0:T(128)}, u32[]{:S(2)}) copy-start(f32[8]{0:T(128)} %copy-done.47) | copy-start | bytes 100
  231.3 12.1 %copy-start.50 = (f32[8]{0:T(128)S(1)}, f32[8]{0:T(128)}, u32[]{:S(2)}) copy-start(f32[8]{0:T(128)} %exp.133) | copy-start | bytes 100
  232.1 10.4 %all-to-all-start.1 = ((bf16[2,16,2,512]{3,0,2,1:T(2,128)(2,1)}), bf16[2,16,2,512]{3,0,2,1:T(2,128)(2,1)S(1)}, u32[]{:S(2)}, u32[]{:S(2)}) async-start(bf16[2,16,2,512]{3,0,2,1:T(2,128)(2,1)} %copy.181), calls=%async_computation.1 | async-start | bytes 131072 | tf_op jit(solution)/shard_map/all_to_all | solution.py:258
  235.7 81.0 %all-gather.21.cloned.1.call-start = ((), (), s32[]{:S(2)}) async-start(), calls=%async_computation.3 | async-start | bytes 2228224 | tf_op jit(solution)/shard_map/all_gather | solution.py:14
  236.2 74.2 %copy-start.56 = (bf16[2,8]{1,0:T(2,128)(2,1)S(1)}, bf16[2,8]{1,0:T(2,128)(2,1)}, u32[]{:S(2)}) copy-start(bf16[2,8]{1,0:T(2,128)(2,1)} %copy-done.55) | copy-start | bytes 100
  237.1 117.6 %all-gather.25.cloned.1.call-start = ((), (), s32[]{:S(2)}) async-start(), calls=%async_computation.5 | async-start | bytes 2228224 | tf_op jit(solution)/shard_map/all_gather | solution.py:14
  310.4 0.7 copy-start.14
  310.4 0.7 copy-start.42
  310.4 5.9 %copy-start.54 = (bf16[2,8]{1,0:T(2,128)(2,1)S(1)}, bf16[2,8]{1,0:T(2,128)(2,1)}, u32[]{:S(2)}) copy-start(bf16[2,8]{1,0:T(2,128)(2,1)} %copy-done.53) | copy-start | bytes 100
  316.3 0.6 copy-start.30
  316.9 30.1 %copy-start.12 = (f32[64,8]{0,1:T(8,128)S(1)}, f32[64,8]{0,1:T(8,128)}, u32[]{:S(2)}) copy-start(f32[64,8]{0,1:T(8,128)} %copy-done.10) | copy-start | bytes 6148
  316.9 31.4 %copy-start.3 = (bf16[512,512]{1,0:T(8,128)(2,1)S(1)}, bf16[512,512]{1,0:T(8,128)(2,1)}, u32[]{:S(2)}) copy-start(bf16[512,512]{1,0:T(8,128)(2,1)} %param.50) | copy-start | bytes 1572868
  316.9 37.8 %copy-start.29 = (f32[8]{0:T(128)S(1)}, f32[8]{0:T(128)}, u32[]{:S(2)}) copy-start(f32[8]{0:T(128)} %custom-call.9) | copy-start | bytes 100
  354.7 30.5 %copy-start.4 = (bf16[1,2,32,512]{3,2,1,0:T(8,128)(2,1)S(1)}, bf16[1,2,32,512]{3,2,1,0:T(8,128)(2,1)}, u32[]{:S(2)}) copy-start(bf16[1,2,32,512]{3,2,1,0:T(8,128)(2,1)} %param.38) | copy-start | bytes 196612
  354.7 30.5 %copy-start.35 = (f32[512]{0:T(512)S(1)}, f32[512]{0:T(512)}, u32[]{:S(2)}) copy-start(f32[512]{0:T(512)} %param.41) | copy-start | bytes 6148
  354.7 30.9 %copy-start.44 = (f32[64]{0:T(128)S(1)}, f32[64]{0:T(128)}, u32[]{:S(2)}) copy-start(f32[64]{0:T(128)} %copy-done.43) | copy-start | bytes 772
  354.7 30.9 %copy-start.49 = (f32[64]{0:T(128)S(1)}, f32[64]{0:T(128)}, u32[]{:S(2)}) copy-start(f32[64]{0:T(128)} %multiply_multiply_fusion) | copy-start | bytes 772
Sparse Core Ops, SparseCore 0:
  51.7 39.1 all-gather.22
  93.0 40.8 all-gather.18
  238.7 43.0 all-gather.20
  316.8 37.8 all-gather.24
where the time goes:
time: 397 us; the launch traced here: 393 us
  blocking collectives  183 us (46%)
  local copies, waits for them, and re-layouts  79.5 us (20%)
  other arithmetic  66.4 us (17%)
  matrix products  20.7 us (5%)
  between operations  16.2 us (4%)
  waiting for transfers between devices  15.7 us (4%)
  starting transfers between devices  7.17 us (2%)
  loops' own time  4.28 us (1%)
    unnamed x3, blocking collectives  102 us
    dynamic_slice x128, local copies, waits for them, and re-layouts, lap(): new = combine(before, jax.tree.map(lambda part: part[at], everything))  66.8 us
    psum x1, blocking collectives, carry_chain(): group_state, group_spent = lax.psum((decayed, spent), 'seq')  60.8 us
    select_n x192, other arithmetic, lap(): return jax.tree.map(lambda a, b: jnp.where(reached, a, b), new, before)  60.4 us
    all_gather x4, blocking collectives, carried_in(): lax.all_gather(a.astype(kind), axis)  20 us
  transfers between devices with their start and end apart: 6, of which 3 were waited for; matrix products, arithmetic and copies ran while one was open for 18% of the time, Pallas kernels for 0%

commit v1 on v0

v1 whole, which is shorter than its diff:
```python
import functools

import jax
import jax.numpy as jnp
import numpy as np
from jax import lax
from jax.experimental import pallas as pl
from jax.experimental.pallas import tpu as pltpu
from jax.sharding import PartitionSpec as P

EPSILON = 1e-05
F32, BF16 = jnp.float32, jnp.bfloat16
HIGH = lax.Precision.HIGHEST
LANES = 128
PACK = 16


def mm(a, b, ca=1, cb=0, precision=None):
    return lax.dot_general(
        a, b, (((ca,), (cb,)), ((), ())), preferred_element_type=F32, precision=precision
    )


def one_minus_exp(y):
    near = jnp.maximum(y, -0.5)
    series = 1.0 + near * (1.0 / 9.0)
    for k in range(8, 1, -1):
        series = 1.0 + near * (1.0 / k) * series
    return jnp.where(y > -0.5, -near * series, 1.0 - jnp.exp(y))


def constants(T, heads, width, row_share, col_share, peers):
    rows, cols = peers * row_share, peers * col_share
    model = heads * width
    t = np.arange(T)
    tri = (t[:, None] >= t[None, :]).astype(np.float32)
    eye = np.eye(T, dtype=np.float32)
    lane = np.arange(model)
    expand = (lane[None, :] // width == np.arange(heads)[:, None]).astype(np.float32)
    s = np.arange(width)
    diag = (lane[None, :] % width == s[:, None]).astype(np.float32)
    quad = min(4, heads)
    q = np.arange(quad * width) // width
    block = (q[:, None] == q[None, :]).astype(np.float32)
    share = row_share * col_share
    parts = max(1, PACK // share)
    o = np.arange(peers * parts * share)
    d, j, c, r = o // (parts * share), o // share % parts, o // row_share % col_share, o % row_share
    row_from = j * T + r * cols + d * col_share + c
    col_from = j * T + c * rows + d * row_share + r
    i = np.arange(parts * T)
    pack_row = (row_from[:, None] == i[None, :]).astype(np.float32)
    pack_col = (col_from[:, None] == i[None, :]).astype(np.float32)
    as16 = lambda a: jnp.asarray(a.astype(np.float32), BF16)
    return (
        jnp.asarray(tri),
        jnp.asarray(eye),
        jnp.asarray(expand),
        jnp.asarray(diag),
        as16(block),
        as16(pack_row),
        as16(pack_col),
        as16(pack_row.T),
        as16(pack_col.T),
    ), parts


def kernel(
    sizes,
    tokens,
    row_select,
    row_decay,
    row_gain,
    row_skip,
    row_in,
    row_out,
    col_select,
    col_decay,
    col_gain,
    col_skip,
    col_in,
    col_out,
    cotangent,
    tri,
    eye,
    expand,
    diag,
    block,
    pack_row,
    pack_col,
    open_row,
    open_col,
    mixed,
    grad_tokens,
    cum_ref,
    inw_ref,
    scan_ref,
    dec_out,
    dec_in,
    state_out,
    state_in,
    inner,
    frame_in,
    enter_out,
    enter_in,
    swap_out,
    swap_in,
    send_sem,
    recv_sem,
):
    peers, frames, heads, width, parts = sizes
    T, model = tokens.shape
    half = row_select.shape[1] // 2
    blocks = T // width
    me, frame = lax.axis_index("seq"), lax.axis_index("frame")
    strips, halves = model // LANES, half // PACK
    tiles = 2 * strips * halves

    barrier = pltpu.get_barrier_semaphore()

    def greet(o, axis, here, count):
        there = lax.rem(here + o, count)
        pl.semaphore_signal(
            barrier, inc=1, device_id={axis: there}, device_id_type=pl.DeviceIdType.MESH
        )

    lax.fori_loop(1, peers, lambda o, _: (greet(o, "seq", me, peers), 0)[1], 0)
    lax.fori_loop(1, frames, lambda o, _: (greet(o, "frame", frame, frames), 0)[1], 0)

    def remote(src, dst, at, axis, there):
        return pltpu.make_async_remote_copy(
            src_ref=src,
            dst_ref=dst,
            send_sem=send_sem.at[at],
            recv_sem=recv_sem.at[at],
            device_id={axis: there},
            device_id_type=pl.DeviceIdType.MESH,
        )

    def to_peers(src_of, dst, at, owners):
        def one(o, _):
            there = lax.rem(me + o, peers)
            copy = remote(src_of(there), dst.at[me], at, "seq", there)
            if owners and tiles < peers:
                pl.when(there < tiles)(copy.start)
            else:
                copy.start()
            return 0

        lax.fori_loop(1, peers, one, 0)

    def only_owner(do):
        if tiles < peers:
            pl.when(me < tiles)(do)
        else:
            do()

    def arrived(ref, at, count):
        part = ref.at[pl.ds(0, count)]
        pltpu.make_async_copy(part, part, recv_sem.at[at]).wait()

    def sent(ref, at, count):
        def one(_, c):
            pltpu.make_async_copy(ref.at[0], ref.at[0], send_sem.at[at]).wait()
            return c

        lax.fori_loop(0, count, one, 0)

    def decays(m, decay):
        cols = decay.shape[2]
        cum = jnp.zeros((T, heads), F32)
        lam = jnp.zeros((T, heads), F32)
        for r in range(decay.shape[1]):
            piece = decay[:, r, :]
            cum += mm(tri[:, r * cols : (r + 1) * cols], piece, 1, 1, HIGH)
            lam += mm(eye[:, r * cols : (r + 1) * cols], piece, 1, 1, HIGH)
        inward = jnp.sqrt(one_minus_exp(2.0 * lam))
        cum_ref[m] = mm(cum, expand[...], 1, 0, HIGH)
        inw_ref[m] = mm(inward, expand[...], 1, 0, HIGH)

    decays(0, row_decay)
    decays(1, col_decay)
    for m in range(2):
        for j in range(strips):
            dec_out[j, m : m + 1, :] = cum_ref[m, T - 1 : T, j * LANES : (j + 1) * LANES]

    pl.semaphore_wait(barrier, peers - 1 + frames - 1)
    to_peers(lambda there: dec_out.at[lax.rem(there, strips)], dec_in, 0, True)
    dec_in[me] = dec_out[lax.rem(me, strips)]

    def vectors(select):
        both = select[...].astype(F32)
        return both[:, :half].astype(BF16), both[:, half:].astype(BF16)

    picks = (vectors(row_select), vectors(col_select))

    def skip_of(ref):
        return mm(ref[...], expand[...], 1, 0, HIGH)

    skips = (skip_of(row_skip), skip_of(col_skip))

    def decay_to_end(m):
        return jnp.exp(cum_ref[m, T - 1 : T, :] - cum_ref[m]) * inw_ref[m]

    def leaves(m, values, backward):
        factor = jnp.exp(cum_ref[m]) if backward else decay_to_end(m)
        weighted = (values.astype(F32) * factor).astype(BF16)
        return mm(picks[m][1] if backward else picks[m][0], weighted, 0, 0)

    def block_scan(m, slot, b, values, memory, backward):
        at = slice(0, T) if blocks == 1 else pl.ds(pl.multiple_of(b * width, width), width)
        cum, inw = cum_ref[m, at, :], inw_ref[m, at, :]
        spread = jnp.sum(cum * diag[...], axis=0, keepdims=True)
        if blocks == 1:
            b_vec, c_vec = picks[m]
            mine = values
        else:
            both = (col_select if m else row_select)[at, :].astype(F32)
            b_vec, c_vec = both[:, :half].astype(BF16), both[:, half:].astype(BF16)
            mine = scan_ref[slot, at, :].astype(BF16)
        position = lax.broadcasted_iota(jnp.int32, (width, model), 0)
        lane = lax.broadcasted_iota(jnp.int32, (width, model), 1) & (width - 1)
        many = lambda v: jnp.concatenate([v] * heads, axis=0)
        if backward:
            gap, kept = spread - cum, lane >= position
            affinity = mm(b_vec, many(c_vec), 1, 1)
            inward = inw
        else:
            gap, kept = cum - spread, lane <= position
            affinity = mm(c_vec, many(b_vec), 1, 1)
            inward = jnp.sum(inw * diag[...], axis=0, keepdims=True)
        decayed = jnp.exp(jnp.minimum(gap, 0.0)) * affinity * inward
        mixing = jnp.where(kept, decayed, 0.0).astype(BF16)
        wide = block.shape[0]
        pieces = []
        for q in range(model // wide):
            v = mine[:, q * wide : (q + 1) * wide]
            stacked = jnp.concatenate([v] * (wide // width), axis=0) * block[...]
            pieces.append(mm(mixing[:, q * wide : (q + 1) * wide], stacked))
        result = jnp.concatenate(pieces, axis=1) + skips[m] * mine.astype(F32)
        if blocks == 1:
            scan_ref[slot] = result
            return memory
        last = cum[width - 1 : width, :]
        before = jnp.sum(jnp.where(position == 0, cum - lam_of(m, b), 0.0), axis=0, keepdims=True)
        opening, ending = jnp.exp(cum - before), jnp.exp(last - cum) * inw
        read, write = (b_vec, c_vec) if backward else (c_vec, b_vec)
        outer, inner_factor = (ending, opening) if backward else (opening, ending)
        result += mm(read.astype(F32), memory, 1, 0, HIGH) * outer
        scan_ref[slot, at, :] = result
        weighted = (mine.astype(F32) * inner_factor).astype(BF16)
        return jnp.exp(last - before) * memory + mm(write, weighted, 0, 0)

    def lam_of(m, b):
        at = pl.multiple_of(b * width, width)
        here = cum_ref[m, pl.ds(at, width), :][0:1, :]
        prior_at = pl.multiple_of(jnp.maximum(b - 1, 0) * width, width)
        prior = cum_ref[m, pl.ds(prior_at, width), :][width - 1 : width, :]
        return here - jnp.where(b > 0, prior, 0.0)

    def local_scan(m, slot, values, backward):
        zero = jnp.zeros((half, model), F32)
        if blocks == 1:
            block_scan(m, slot, 0, values, zero, backward)
            return
        scan_ref[slot] = values.astype(F32)
        lax.fori_loop(
            0,
            blocks,
            lambda i, memory: block_scan(
                m, slot, (blocks - 1 - i) if backward else i, None, memory, backward
            ),
            zero,
        )

    def stage(e, a, state):
        for i in range(halves):
            for j in range(strips):
                state_out[e, (a * halves + i) * strips + j] = state[
                    i * PACK : (i + 1) * PACK, j * LANES : (j + 1) * LANES
                ].astype(BF16)

    def send_states(e):
        to_peers(lambda there: state_out.at[e, there], state_in.at[e], 1 + 4 * e, True)

        def keep():
            state_in[e, me] = state_out[e, me]

        only_owner(keep)

    def own(e):
        at = 1 + 4 * e
        back = me >= tiles // 2
        if e == 0:
            arrived(dec_in, 0, peers - 1)
        arrived(state_in.at[e], at, peers - 1)
        second = back if e == 0 else jnp.logical_not(back)
        memory = jnp.zeros((PACK, LANES), F32)
        total = jnp.zeros((1, LANES), F32)
        totals = []
        for i in range(peers):
            p = jnp.where(back, peers - 1 - i, i)
            pair = dec_in[p]
            spent = jnp.where(second, pair[1:2, :], pair[0:1, :])
            inner[i] = memory
            totals.append(total)
            memory = jnp.exp(spent) * memory + state_in[e, p].astype(F32)
            total = total + spent
        frame_in[e, frame, 0:PACK, :] = memory
        frame_in[e, frame, PACK : PACK + 8, :] = jnp.broadcast_to(total, (8, LANES))

        def one(o, _):
            there = lax.rem(frame + o, frames)
            remote(frame_in.at[e, frame], frame_in.at[e, frame], at + 1, "frame", there).start()
            return 0

        lax.fori_loop(1, frames, one, 0)
        arrived(frame_in.at[e], at + 1, frames - 1)
        carry = jnp.zeros((PACK, LANES), F32)
        for i in range(frames - 1):
            g = jnp.where(back, frames - 1 - i, i)
            reached = jnp.where(back, g > frame, g < frame)
            new = jnp.exp(frame_in[e, g, PACK : PACK + 1, :]) * carry + frame_in[e, g, 0:PACK, :]
            carry = jnp.where(reached, new, carry)
        for i in range(peers):
            p = jnp.where(back, peers - 1 - i, i)
            enter_out[e, p] = (inner[i] + jnp.exp(totals[i]) * carry).astype(BF16)
        to_peers(lambda there: enter_out.at[e, there], enter_in.at[e], at + 2, False)
        enter_in[e, me] = enter_out[e, me]

    def entering(e):
        if tiles < peers:
            pl.when(me < tiles)(lambda: arrived(enter_in.at[e], 3 + 4 * e, tiles - 1))
            pl.when(me >= tiles)(lambda: arrived(enter_in.at[e], 3 + 4 * e, tiles))
        else:
            arrived(enter_in.at[e], 3 + 4 * e, tiles - 1)
        return tuple(
            jnp.concatenate(
                [
                    jnp.concatenate(
                        [enter_in[e, (a * halves + i) * strips + j] for j in range(strips)], axis=1
                    )
                    for i in range(halves)
                ],
                axis=0,
            )
            for a in range(2)
        )

    def finish_scan(m, slot, state, backward):
        if backward:
            carried = mm(picks[m][0], state) * decay_to_end(m)
        else:
            carried = mm(picks[m][1], state) * jnp.exp(cum_ref[m])
        return (scan_ref[slot] + carried).astype(BF16)

    def factor_of(floats):
        return lax.rsqrt(jnp.mean(floats * floats, axis=-1, keepdims=True) + EPSILON)

    def project(values, gain, weight):
        floats = values.astype(F32)
        normed = (floats * factor_of(floats) * gain[...]).astype(BF16)
        return mm(normed, weight[...]).astype(BF16)

    def input_gradient(values, incoming, scanned, gain, weight):
        returned = mm(scanned, weight[...], 1, 1)
        floats = values.astype(F32)
        factor = factor_of(floats)
        scaled = gain[...] * returned
        inner_mean = jnp.mean(scaled * floats, axis=-1, keepdims=True)
        result = incoming.astype(F32) + factor * scaled - floats * (factor**3 * inner_mean)
        return result.astype(BF16)

    strip = model // parts
    share = T // peers * parts

    def swap_send(e, values, pack):
        stacked = jnp.concatenate(
            [values[:, j * strip : (j + 1) * strip] for j in range(parts)], axis=0
        )
        packed = mm(pack[...], stacked).astype(BF16)
        swap_out[e] = packed.reshape(peers, share, strip)
        to_peers(lambda there: swap_out.at[e, there], swap_in.at[e], 9 + e, False)
        swap_in[e, me] = swap_out[e, me]

    def swap_take(e, pack):
        arrived(swap_in.at[e], 9 + e, peers - 1)
        packed = swap_in[e].reshape(peers * share, strip)
        stacked = mm(pack[...], packed).astype(BF16)
        return jnp.concatenate([stacked[j * T : (j + 1) * T, :] for j in range(parts)], axis=1)

    def ends(m, slot, values, backward):
        return leaves(m, values, backward)

    row_values = project(tokens[...], row_gain, row_in)
    stage(0, 0, ends(0, 0, row_values, False))
    col_pulled = mm(cotangent[...], col_out[...], 1, 1).astype(BF16)
    stage(0, 1, ends(1, 1, col_pulled, True))
    send_states(0)
    local_scan(0, 0, row_values, False)
    local_scan(1, 1, col_pulled, True)
    only_owner(lambda: own(0))
    row_state, col_state = entering(0)
    row_scanned = finish_scan(0, 0, row_state, False)
    row_mixed = (tokens[...].astype(F32) + mm(row_scanned, row_out[...])).astype(BF16)
    swap_send(0, row_mixed, pack_row)
    col_scanned = finish_scan(1, 1, col_state, True)
    col_tokens = swap_take(0, open_col)
    col_grad = input_gradient(col_tokens, cotangent[...], col_scanned, col_gain, col_in)
    swap_send(1, col_grad, pack_col)
    col_values = project(col_tokens, col_gain, col_in)
    stage(1, 0, ends(1, 0, col_values, False))
    local_scan(1, 0, col_values, False)
    row_grad = swap_take(1, open_row)
    row_pulled = mm(row_grad, row_out[...], 1, 1).astype(BF16)
    stage(1, 1, ends(0, 1, row_pulled, True))
    send_states(1)
    local_scan(0, 1, row_pulled, True)
    only_owner(lambda: own(1))
    col_state, row_state = entering(1)
    col_scanned = finish_scan(1, 0, col_state, False)
    mixed[...] = (col_tokens.astype(F32) + mm(col_scanned, col_out[...])).astype(BF16)
    row_scanned = finish_scan(0, 1, row_state, True)
    grad_tokens[...] = input_gradient(tokens[...], row_grad, row_scanned, row_gain, row_in)

    def drain(ref, at, owners):
        if owners and tiles < peers:
            pl.when(me < tiles)(lambda: sent(ref, at, tiles - 1))
            pl.when(me >= tiles)(lambda: sent(ref, at, tiles))
        else:
            sent(ref, at, peers - 1)

    drain(dec_out, 0, True)
    for e in range(2):
        drain(state_out.at[e], 1 + 4 * e, True)
        only_owner(lambda: sent(frame_in.at[e], 2 + 4 * e, frames - 1))
        only_owner(lambda: sent(enter_out.at[e], 3 + 4 * e, peers - 1))
        drain(swap_out.at[e], 9 + e, False)


def body(peers, frames, tokens, row_select, row_decay, row_gain, row_skip, row_in, row_out,
         col_select, col_decay, col_gain, col_skip, col_in, col_out, cotangent):
    model = tokens.shape[-1]
    heads = row_decay.shape[1]
    doubled = row_select.shape[-1]
    half = doubled // 2
    width = model // heads
    flat = tokens.reshape(-1, model)
    T = flat.shape[0]
    fixed, parts = constants(
        T, heads, width, row_decay.shape[2], col_decay.shape[2], peers
    )
    strips = model // LANES
    tiles = 2 * strips * (half // PACK)
    vmem = pl.BlockSpec(memory_space=pltpu.VMEM)
    share = T // peers * parts
    operands = (
        flat,
        row_select.reshape(-1, doubled),
        row_decay.reshape(row_decay.shape[1:]),
        row_gain.reshape(1, -1),
        row_skip.reshape(1, -1),
        row_in,
        row_out,
        col_select.reshape(-1, doubled),
        col_decay.reshape(col_decay.shape[1:]),
        col_gain.reshape(1, -1),
        col_skip.reshape(1, -1),
        col_in,
        col_out,
        cotangent.reshape(-1, model),
    ) + fixed
    out = jax.ShapeDtypeStruct((T, model), BF16)
    mixed, grad = pl.pallas_call(
        functools.partial(kernel, (peers, frames, heads, width, parts)),
        out_shape=(out, out),
        in_specs=[vmem] * len(operands),
        out_specs=(vmem, vmem),
        scratch_shapes=[
            pltpu.VMEM((2, T, model), F32),
            pltpu.VMEM((2, T, model), F32),
            pltpu.VMEM((2, T, model), F32),
            pltpu.VMEM((strips, 2, LANES), F32),
            pltpu.VMEM((peers, 2, LANES), F32),
            pltpu.VMEM((2, tiles, PACK, LANES), BF16),
            pltpu.VMEM((2, peers, PACK, LANES), BF16),
            pltpu.VMEM((peers, PACK, LANES), F32),
            pltpu.VMEM((2, frames, PACK + 8, LANES), F32),
            pltpu.VMEM((2, peers, PACK, LANES), BF16),
            pltpu.VMEM((2, tiles, PACK, LANES), BF16),
            pltpu.VMEM((2, peers, share, model // parts), BF16),
            pltpu.VMEM((2, peers, share, model // parts), BF16),
            pltpu.SemaphoreType.DMA((11,)),
            pltpu.SemaphoreType.DMA((11,)),
        ],
        compiler_params=pltpu.CompilerParams(
            collective_id=0, has_side_effects=True, vmem_limit_bytes=48 * 1024 * 1024
        ),
    )(*operands)
    return (mixed.reshape(cotangent.shape), grad.reshape(tokens.shape))


def solution(mesh):
    token, decay = P("frame", "seq", None, None), P("frame", None, "seq", None)
    mixer = (token, decay, P(), P(), P(), P())
    return jax.shard_map(
        functools.partial(body, mesh.shape["seq"], mesh.shape["frame"]),
        mesh=mesh,
        in_specs=(token,) + mixer + mixer + (token,),
        out_specs=(token, token),
        check_vma=False,
    )
```

time: 397 us -> 60.8 us (0.15)
  blocking collectives: 183 us -> 0 us
  other arithmetic: 66.4 us -> 0 us
  local copies, waits for them, and re-layouts: 79.5 us -> 18.9 us
  Pallas kernels: 0 us -> 40.3 us
  matrix products: 20.7 us -> 0 us
  waiting for transfers between devices: 15.7 us -> 0 us
  between operations: 16.2 us -> 0.69 us
  starting transfers between devices: 7.17 us -> 0 us
  loops' own time: 4.28 us -> 0 us
    unnamed x3 -> x0, blocking collectives: 102 us -> none
    dynamic_slice x132 -> x0, local copies, waits for them, and re-layouts: 67 us -> none  [the longest x128 66.8 us: lap(): new = combine(before, jax.tree.map(lambda part: part[at], everything))]
    psum x1 -> x0, blocking collectives: 60.8 us -> none  [carry_chain(): group_state, group_spent = lax.psum((decayed, spent), 'seq')]
    select_n x192 -> x0, other arithmetic: 60.4 us -> none  [lap(): return jax.tree.map(lambda a, b: jnp.where(reached, a, b), new, before)]
    pallas_call x0 -> x1, Pallas kernels: none -> 40.3 us  [body(): pl.pallas_call(functools.partial(kernel, (peers, frames, heads, width, pa...]
    dot_general x26 -> x0, matrix products: 20.7 us -> none  [the longest x2 2.68 us: backward_block(): jnp.einsum('thp,tn->hpn', weighted, select_block[:, half_width:], preferr...]
    all_gather x4 -> x0, blocking collectives: 20 us -> none  [carried_in(): lax.all_gather(a.astype(kind), axis)]
    unnamed x130 -> x48, local copies, waits for them, and re-layouts: 5.73 us -> 18.9 us
  transfers between devices with their start and end apart: 6 -> 0, of which waited for: 3 -> 0; matrix products, arithmetic and copies ran while one was open for 18% -> 0% of each run, Pallas kernels for 0% -> 0%
where the time goes in v1:
time: 60.8 us; the launch traced here: 59.9 us
  Pallas kernels  40.3 us (66%)
  local copies, waits for them, and re-layouts  18.9 us (31%)
  between operations  0.69 us (1%)
    pallas_call x1, Pallas kernels, body(): pl.pallas_call(functools.partial(kernel, (peers, frames, heads, width, pa...  40.3 us
    unnamed x48, local copies, waits for them, and re-layouts  18.9 us

profile of v1, /device:TPU:0, one launch (start us, length us, event | category | flops | bytes accessed | tf_op | source)
XLA Modules:
  0.0 59.9 jit_solution(12609969429491220227)
XLA Ops:
  0.6 0.0 copy-start.14
  0.6 0.0 copy-start.19
  0.7 0.0 copy-start.21
  0.7 0.7 %copy-done.14 = bf16[1,2,32,64]{3,2,1,0:T(8,128)(2,1)S(1)} copy-done((bf16[1,2,32,64]{3,2,1,0:T(8,128)(2,1)S(1)}, bf16[1,2,32,64]{3,2,1,0:T(8,128)(2,1)}, u32[]{:S(2)}) %copy-start.14) | copy-done | bytes 8216
  1.4 0.0 copy-done.19
  1.4 0.0 copy-done.21
  1.4 0.0 copy-start
  1.4 1.0 %copy-done = bf16[512,512]{1,0:T(8,128)(2,1)S(1)} copy-done((bf16[512,512]{1,0:T(8,128)(2,1)S(1)}, bf16[512,512]{1,0:T(8,128)(2,1)}, u32[]{:S(2)}) %copy-start) | copy-done | bytes 524312
  2.4 0.0 copy-start.1
  2.4 1.0 %copy-done.1 = bf16[512,512]{1,0:T(8,128)(2,1)S(1)} copy-done((bf16[512,512]{1,0:T(8,128)(2,1)S(1)}, bf16[512,512]{1,0:T(8,128)(2,1)}, u32[]{:S(2)}) %copy-start.1) | copy-done | bytes 524312
  3.4 0.0 copy-start.2
  3.4 1.0 %copy-done.2 = bf16[512,512]{1,0:T(8,128)(2,1)S(1)} copy-done((bf16[512,512]{1,0:T(8,128)(2,1)S(1)}, bf16[512,512]{1,0:T(8,128)(2,1)}, u32[]{:S(2)}) %copy-start.2) | copy-done | bytes 524312
  4.5 0.0 copy-start.3
  4.5 1.0 %copy-done.3 = bf16[512,512]{1,0:T(8,128)(2,1)S(1)} copy-done((bf16[512,512]{1,0:T(8,128)(2,1)S(1)}, bf16[512,512]{1,0:T(8,128)(2,1)}, u32[]{:S(2)}) %copy-start.3) | copy-done | bytes 524312
  5.5 0.0 copy-start.4
  5.5 0.9 %copy-done.4 = bf16[256,256]{1,0:T(8,128)(2,1)S(1)} copy-done((bf16[256,256]{1,0:T(8,128)(2,1)S(1)}, bf16[256,256]{1,0:T(8,128)(2,1)}, u32[]{:S(2)}) %copy-start.4) | copy-done | bytes 131096
  6.4 0.0 copy-start.5
  6.4 0.9 %copy-done.5 = bf16[256,256]{1,0:T(8,128)(2,1)S(1)} copy-done((bf16[256,256]{1,0:T(8,128)(2,1)S(1)}, bf16[256,256]{1,0:T(8,128)(2,1)}, u32[]{:S(2)}) %copy-start.5) | copy-done | bytes 131096
  7.3 0.0 copy-start.6
  7.3 0.9 %copy-done.6 = bf16[256,256]{1,0:T(8,128)(2,1)S(1)} copy-done((bf16[256,256]{1,0:T(8,128)(2,1)S(1)}, bf16[256,256]{1,0:T(8,128)(2,1)}, u32[]{:S(2)}) %copy-start.6) | copy-done | bytes 131096
  8.2 0.0 copy-start.7
  8.2 0.9 %copy-done.7 = bf16[256,256]{1,0:T(8,128)(2,1)S(1)} copy-done((bf16[256,256]{1,0:T(8,128)(2,1)S(1)}, bf16[256,256]{1,0:T(8,128)(2,1)}, u32[]{:S(2)}) %copy-start.7) | copy-done | bytes 131096
  9.1 0.0 copy-start.8
  9.2 0.9 %copy-done.8 = bf16[256,256]{1,0:T(8,128)(2,1)S(1)} copy-done((bf16[256,256]{1,0:T(8,128)(2,1)S(1)}, bf16[256,256]{1,0:T(8,128)(2,1)}, u32[]{:S(2)}) %copy-start.8) | copy-done | bytes 131096
  10.1 0.0 copy-start.9
  10.1 0.9 %copy-done.9 = f32[64,512]{1,0:T(8,128)S(1)} copy-done((f32[64,512]{1,0:T(8,128)S(1)}, f32[64,512]{1,0:T(8,128)}, u32[]{:S(2)}) %copy-start.9) | copy-done | bytes 131096
  11.0 0.0 copy-start.10
  11.0 0.8 %copy-done.10 = bf16[1,2,32,512]{3,2,1,0:T(8,128)(2,1)S(1)} copy-done((bf16[1,2,32,512]{3,2,1,0:T(8,128)(2,1)S(1)}, bf16[1,2,32,512]{3,2,1,0:T(8,128)(2,1)}, u32[]{:S(2)}) %copy-start.10) | copy-done | bytes 65560
  11.8 0.0 copy-start.11
  11.8 0.8 %copy-done.11 = bf16[1,2,32,512]{3,2,1,0:T(8,128)(2,1)S(1)} copy-done((bf16[1,2,32,512]{3,2,1,0:T(8,128)(2,1)S(1)}, bf16[1,2,32,512]{3,2,1,0:T(8,128)(2,1)}, u32[]{:S(2)}) %copy-start.11) | copy-done | bytes 65560
  12.6 0.0 copy-start.12
  12.6 0.8 %copy-done.12 = f32[64,64]{1,0:T(8,128)S(1)} copy-done((f32[64,64]{1,0:T(8,128)S(1)}, f32[64,64]{1,0:T(8,128)}, u32[]{:S(2)}) %copy-start.12) | copy-done | bytes 16408
  13.4 0.0 copy-start.13
  13.4 0.8 %copy-done.13 = f32[64,64]{1,0:T(8,128)S(1)} copy-done((f32[64,64]{1,0:T(8,128)S(1)}, f32[64,64]{1,0:T(8,128)}, u32[]{:S(2)}) %copy-start.13) | copy-done | bytes 16408
  14.2 0.0 copy-start.15
  14.2 0.7 %copy-done.15 = bf16[1,2,32,64]{3,2,1,0:T(8,128)(2,1)S(1)} copy-done((bf16[1,2,32,64]{3,2,1,0:T(8,128)(2,1)S(1)}, bf16[1,2,32,64]{3,2,1,0:T(8,128)(2,1)}, u32[]{:S(2)}) %copy-start.15) | copy-done | bytes 8216
  14.9 0.0 copy-start.16
  14.9 0.7 %copy-done.16 = f32[8,512]{1,0:T(8,128)S(1)} copy-done((f32[8,512]{1,0:T(8,128)S(1)}, f32[8,512]{1,0:T(8,128)}, u32[]{:S(2)}) %copy-start.16) | copy-done | bytes 16408
  15.6 0.0 copy-start.17
  15.6 0.7 %copy-done.17 = f32[1,8,2,32]{3,2,1,0:T(2,128)S(1)} copy-done((f32[1,8,2,32]{3,2,1,0:T(2,128)S(1)}, f32[1,8,2,32]{3,2,1,0:T(2,128)}, u32[]{:S(2)}) %copy-start.17) | copy-done | bytes 2072
  16.3 0.0 copy-start.18
  16.3 0.7 %copy-done.18 = f32[1,8,2,32]{3,2,1,0:T(2,128)S(1)} copy-done((f32[1,8,2,32]{3,2,1,0:T(2,128)S(1)}, f32[1,8,2,32]{3,2,1,0:T(2,128)}, u32[]{:S(2)}) %copy-start.18) | copy-done | bytes 2072
  17.0 0.0 copy-start.20
  17.0 0.7 %copy-done.20 = f32[512]{0:T(512)S(1)} copy-done((f32[512]{0:T(512)S(1)}, f32[512]{0:T(512)}, u32[]{:S(2)}) %copy-start.20) | copy-done | bytes 2072
  17.7 0.0 copy-start.22
  17.7 0.7 %copy-done.22 = f32[8]{0:T(128)S(1)} copy-done((f32[8]{0:T(128)S(1)}, f32[8]{0:T(128)}, u32[]{:S(2)}) %copy-start.22) | copy-done | bytes 56
  18.3 40.3 %shard_map.230 = (bf16[64,512]{1,0:T(8,128)(2,1)S(1)}, bf16[64,512]{1,0:T(8,128)(2,1)S(1)}) custom-call(bf16[64,512]{1,0:T(8,128)(2,1)S(1)} %bitcast.12, bf16[64,64]{1,0:T(8,128)(2,1)S(1)} %bitcast.16, f32[8,2,32]{2,1,0:T(2,128)S(1)} %bitcast.18, f32[1,512]{1,0:T(1,128)S(1)} %bitcast.20, f32[1,8]{1,0:T(1,128)S(1)} %bitcast.22, bf16[512,512]{1,0:T(8,128)(2,1)S(1)} %copy-done, ...), custom_call_target="tpu_custom_call" | custom-call | tf_op jit(solution)/shard_map/pallas_call | solution.py:474
  58.6 0.6 %copy.27 = bf16[1,2,32,512]{3,2,1,0:T(8,128)(2,1)} copy(bf16[1,2,32,512]{3,2,1,0:T(8,128)(2,1)S(1)} %bitcast.15) | data formatting | bytes 131072
  59.3 0.6 %copy.28 = bf16[1,2,32,512]{3,2,1,0:T(8,128)(2,1)} copy(bf16[1,2,32,512]{3,2,1,0:T(8,128)(2,1)S(1)} %bitcast.14) | data formatting | bytes 131072
Async XLA Ops:
  0.6 0.7 %copy-start.14 = (bf16[1,2,32,64]{3,2,1,0:T(8,128)(2,1)S(1)}, bf16[1,2,32,64]{3,2,1,0:T(8,128)(2,1)}, u32[]{:S(2)}) copy-start(bf16[1,2,32,64]{3,2,1,0:T(8,128)(2,1)} %param.24) | copy-start | bytes 24580
  0.6 0.7 %copy-start.19 = (f32[512]{0:T(512)S(1)}, f32[512]{0:T(512)}, u32[]{:S(2)}) copy-start(f32[512]{0:T(512)} %param.26) | copy-start | bytes 6148
  0.7 0.7 %copy-start.21 = (f32[8]{0:T(128)S(1)}, f32[8]{0:T(128)}, u32[]{:S(2)}) copy-start(f32[8]{0:T(128)} %param.27) | copy-start | bytes 100
  1.4 1.0 %copy-start = (bf16[512,512]{1,0:T(8,128)(2,1)S(1)}, bf16[512,512]{1,0:T(8,128)(2,1)}, u32[]{:S(2)}) copy-start(bf16[512,512]{1,0:T(8,128)(2,1)} %row_in.1) | copy-start | bytes 1572868
  2.4 1.0 %copy-start.1 = (bf16[512,512]{1,0:T(8,128)(2,1)S(1)}, bf16[512,512]{1,0:T(8,128)(2,1)}, u32[]{:S(2)}) copy-start(bf16[512,512]{1,0:T(8,128)(2,1)} %row_out.1) | copy-start | bytes 1572868
  3.4 1.0 %copy-start.2 = (bf16[512,512]{1,0:T(8,128)(2,1)S(1)}, bf16[512,512]{1,0:T(8,128)(2,1)}, u32[]{:S(2)}) copy-start(bf16[512,512]{1,0:T(8,128)(2,1)} %col_in.1) | copy-start | bytes 1572868
  4.5 1.0 %copy-start.3 = (bf16[512,512]{1,0:T(8,128)(2,1)S(1)}, bf16[512,512]{1,0:T(8,128)(2,1)}, u32[]{:S(2)}) copy-start(bf16[512,512]{1,0:T(8,128)(2,1)} %col_out.1) | copy-start | bytes 1572868
  5.5 0.9 %copy-start.4 = (bf16[256,256]{1,0:T(8,128)(2,1)S(1)}, bf16[256,256]{1,0:T(8,128)(2,1)}, u32[]{:S(2)}) copy-start(bf16[256,256]{1,0:T(8,128)(2,1)} %constant.26.clone.open_col) | copy-start | bytes 393220
  6.4 0.9 %copy-start.5 = (bf16[256,256]{1,0:T(8,128)(2,1)S(1)}, bf16[256,256]{1,0:T(8,128)(2,1)}, u32[]{:S(2)}) copy-start(bf16[256,256]{1,0:T(8,128)(2,1)} %constant.25.clone.open_row) | copy-start | bytes 393220
  7.3 0.9 %copy-start.6 = (bf16[256,256]{1,0:T(8,128)(2,1)S(1)}, bf16[256,256]{1,0:T(8,128)(2,1)}, u32[]{:S(2)}) copy-start(bf16[256,256]{1,0:T(8,128)(2,1)} %constant.24.clone.pack_col) | copy-start | bytes 393220
  8.2 0.9 %copy-start.7 = (bf16[256,256]{1,0:T(8,128)(2,1)S(1)}, bf16[256,256]{1,0:T(8,128)(2,1)}, u32[]{:S(2)}) copy-start(bf16[256,256]{1,0:T(8,128)(2,1)} %constant.23.clone.pack_row) | copy-start | bytes 393220
  9.1 0.9 %copy-start.8 = (bf16[256,256]{1,0:T(8,128)(2,1)S(1)}, bf16[256,256]{1,0:T(8,128)(2,1)}, u32[]{:S(2)}) copy-start(bf16[256,256]{1,0:T(8,128)(2,1)} %constant.22.clone.block) | copy-start | bytes 393220
  10.1 0.9 %copy-start.9 = (f32[64,512]{1,0:T(8,128)S(1)}, f32[64,512]{1,0:T(8,128)}, u32[]{:S(2)}) copy-start(f32[64,512]{1,0:T(8,128)} %constant.21.clone.diag) | copy-start | bytes 393220
  11.0 0.8 %copy-start.10 = (bf16[1,2,32,512]{3,2,1,0:T(8,128)(2,1)S(1)}, bf16[1,2,32,512]{3,2,1,0:T(8,128)(2,1)}, u32[]{:S(2)}) copy-start(bf16[1,2,32,512]{3,2,1,0:T(8,128)(2,1)} %param.23) | copy-start | bytes 196612
  11.8 0.8 %copy-start.11 = (bf16[1,2,32,512]{3,2,1,0:T(8,128)(2,1)S(1)}, bf16[1,2,32,512]{3,2,1,0:T(8,128)(2,1)}, u32[]{:S(2)}) copy-start(bf16[1,2,32,512]{3,2,1,0:T(8,128)(2,1)} %param.36) | copy-start | bytes 196612
  12.6 0.8 %copy-start.12 = (f32[64,64]{1,0:T(8,128)S(1)}, f32[64,64]{1,0:T(8,128)}, u32[]{:S(2)}) copy-start(f32[64,64]{1,0:T(8,128)} %constant.19.clone.eye) | copy-start | bytes 49156
  13.4 0.8 %copy-start.13 = (f32[64,64]{1,0:T(8,128)S(1)}, f32[64,64]{1,0:T(8,128)}, u32[]{:S(2)}) copy-start(f32[64,64]{1,0:T(8,128)} %constant.18.clone.tri) | copy-start | bytes 49156
  14.2 0.7 %copy-start.15 = (bf16[1,2,32,64]{3,2,1,0:T(8,128)(2,1)S(1)}, bf16[1,2,32,64]{3,2,1,0:T(8,128)(2,1)}, u32[]{:S(2)}) copy-start(bf16[1,2,32,64]{3,2,1,0:T(8,128)(2,1)} %param.30) | copy-start | bytes 24580
  14.9 0.7 %copy-start.16 = (f32[8,512]{1,0:T(8,128)S(1)}, f32[8,512]{1,0:T(8,128)}, u32[]{:S(2)}) copy-start(f32[8,512]{1,0:T(8,128)} %constant.20.clone.expand) | copy-start | bytes 49156
  15.6 0.7 %copy-start.17 = (f32[1,8,2,32]{3,2,1,0:T(2,128)S(1)}, f32[1,8,2,32]{3,2,1,0:T(2,128)}, u32[]{:S(2)}) copy-start(f32[1,8,2,32]{3,2,1,0:T(2,128)} %param.25) | copy-start | bytes 6148
  16.3 0.7 %copy-start.18 = (f32[1,8,2,32]{3,2,1,0:T(2,128)S(1)}, f32[1,8,2,32]{3,2,1,0:T(2,128)}, u32[]{:S(2)}) copy-start(f32[1,8,2,32]{3,2,1,0:T(2,128)} %param.31) | copy-start | bytes 6148
  17.0 0.7 %copy-start.20 = (f32[512]{0:T(512)S(1)}, f32[512]{0:T(512)}, u32[]{:S(2)}) copy-start(f32[512]{0:T(512)} %param.32) | copy-start | bytes 6148
  17.7 0.7 %copy-start.22 = (f32[8]{0:T(128)S(1)}, f32[8]{0:T(128)}, u32[]{:S(2)}) copy-start(f32[8]{0:T(128)} %param.33) | copy-start | bytes 100

commit v2 on v1

--- a/solution.py
+++ b/solution.py
@@ -65,49 +65,117 @@
     ), parts
 
 
-def kernel(
-    sizes,
-    tokens,
-    row_select,
-    row_decay,
-    row_gain,
-    row_skip,
-    row_in,
-    row_out,
-    col_select,
-    col_decay,
-    col_gain,
-    col_skip,
-    col_in,
-    col_out,
-    cotangent,
-    tri,
-    eye,
-    expand,
-    diag,
-    block,
-    pack_row,
-    pack_col,
-    open_row,
-    open_col,
-    mixed,
-    grad_tokens,
-    cum_ref,
-    inw_ref,
-    scan_ref,
-    dec_out,
-    dec_in,
-    state_out,
-    state_in,
-    inner,
-    frame_in,
-    enter_out,
-    enter_in,
-    swap_out,
-    swap_in,
-    send_sem,
-    recv_sem,
-):
+ORDER = (
+    "row_decay",
+    "col_decay",
+    "tri",
+    "eye",
+    "expand",
+    "tokens",
+    "row_gain",
+    "row_in",
+    "row_select",
+    "col_select",
+    "row_skip",
+    "col_skip",
+    "cotangent",
+    "col_out",
+    "diag",
+    "block",
+    "row_out",
+    "pack_row",
+    "open_col",
+    "col_gain",
+    "col_in",
+    "pack_col",
+    "open_row",
+)
+NAMES = (
+    "tokens",
+    "row_select",
+    "row_decay",
+    "row_gain",
+    "row_skip",
+    "row_in",
+    "row_out",
+    "col_select",
+    "col_decay",
+    "col_gain",
+    "col_skip",
+    "col_in",
+    "col_out",
+    "cotangent",
+    "tri",
+    "eye",
+    "expand",
+    "diag",
+    "block",
+    "pack_row",
+    "pack_col",
+    "open_row",
+    "open_col",
+)
+
+
+def kernel(sizes, *refs):
+    count = len(NAMES)
+    far = dict(zip(NAMES, refs[:count]))
+    mixed, grad_tokens = refs[count : count + 2]
+    near = dict(zip(NAMES, refs[count + 2 : 2 * count + 2]))
+    (
+        load_sem,
+        cum_ref,
+        inw_ref,
+        scan_ref,
+        dec_out,
+        dec_in,
+        state_out,
+        state_in,
+        enter_out,
+        enter_in,
+        swap_out,
+        swap_in,
+        send_sem,
+        recv_sem,
+        cross_sem,
+    ) = refs[2 * count + 2 :]
+    loads = {
+        name: pltpu.make_async_copy(far[name], near[name], load_sem.at[i])
+        for i, name in enumerate(ORDER)
+    }
+    for name in ORDER:
+        loads[name].start()
+    ready = iter(ORDER)
+
+    def until(name):
+        for one in ready:
+            loads[one].wait()
+            if one == name:
+                break
+
+    tokens = near["tokens"]
+    row_select = near["row_select"]
+    row_decay = near["row_decay"]
+    row_gain = near["row_gain"]
+    row_skip = near["row_skip"]
+    row_in = near["row_in"]
+    row_out = near["row_out"]
+    col_select = near["col_select"]
+    col_decay = near["col_decay"]
+    col_gain = near["col_gain"]
+    col_skip = near["col_skip"]
+    col_in = near["col_in"]
+    col_out = near["col_out"]
+    cotangent = near["cotangent"]
+    tri = near["tri"]
+    eye = near["eye"]
+    expand = near["expand"]
+    diag = near["diag"]
+    block = near["block"]
+    pack_row = near["pack_row"]
+    pack_col = near["pack_col"]
+    open_row = near["open_row"]
+    open_col = near["open_col"]
     peers, frames, heads, width, parts = sizes
     T, model = tokens.shape
     half = row_select.shape[1] // 2
@@ -125,7 +193,22 @@
         )
 
     lax.fori_loop(1, peers, lambda o, _: (greet(o, "seq", me, peers), 0)[1], 0)
-    lax.fori_loop(1, frames, lambda o, _: (greet(o, "frame", frame, frames), 0)[1], 0)
+
+    def greet_frame(o, _):
+        there = lax.rem(frame + o, frames)
+
+        def one(s, c):
+            pl.semaphore_signal(
+                barrier,
+                inc=1,
+                device_id={"seq": s, "frame": there},
+                device_id_type=pl.DeviceIdType.MESH,
+            )
+            return c
+
+        return lax.fori_loop(0, peers, one, 0)
+
+    lax.fori_loop(1, frames, greet_frame, 0)
 
     def remote(src, dst, at, axis, there):
         return pltpu.make_async_remote_copy(
@@ -149,6 +232,28 @@
 
         lax.fori_loop(1, peers, one, 0)
 
+    def to_frames(src_of, dst, at, slot):
+        def one(o, _):
+            there = lax.rem(frame + o, frames)
+            base = jnp.where(there > frame, 0, tiles // 2)
+
+            def owner(i, c):
+                k = base + lax.rem(me + i, tiles // 2)
+                pltpu.make_async_remote_copy(
+                    src_ref=src_of(k),
+                    dst_ref=dst.at[frame, me],
+                    send_sem=send_sem.at[at],
+                    recv_sem=cross_sem.at[slot, frame],
+                    device_id={"seq": k, "frame": there},
+                    device_id_type=pl.DeviceIdType.MESH,
+                ).start()
+                return c
+
+            lax.fori_loop(0, tiles // 2, owner, 0)
+            return 0
+
+        lax.fori_loop(1, frames, one, 0)
+
     def only_owner(do):
         if tiles < peers:
             pl.when(me < tiles)(do)
@@ -158,6 +263,9 @@
     def arrived(ref, at, count):
         part = ref.at[pl.ds(0, count)]
         pltpu.make_async_copy(part, part, recv_sem.at[at]).wait()
+
+    def all_of(ref, sem):
+        pltpu.make_async_copy(ref, ref, sem).wait()
 
     def sent(ref, at, count):
         def one(_, c):
@@ -178,15 +286,20 @@
         cum_ref[m] = mm(cum, expand[...], 1, 0, HIGH)
         inw_ref[m] = mm(inward, expand[...], 1, 0, HIGH)
 
+    until("expand")
     decays(0, row_decay)
     decays(1, col_decay)
     for m in range(2):
         for j in range(strips):
             dec_out[j, m : m + 1, :] = cum_ref[m, T - 1 : T, j * LANES : (j + 1) * LANES]
 
-    pl.semaphore_wait(barrier, peers - 1 + frames - 1)
-    to_peers(lambda there: dec_out.at[lax.rem(there, strips)], dec_in, 0, True)
-    dec_in[me] = dec_out[lax.rem(me, strips)]
+    pl.semaphore_wait(barrier, peers * frames - 1)
+    strip_of = lambda there: dec_out.at[lax.rem(there, strips)]
+    to_peers(strip_of, dec_in.at[frame], 0, True)
+    to_frames(strip_of, dec_in, 0, 2)
+    dec_in[frame, me] = dec_out[lax.rem(me, strips)]
+
+    until("col_skip")
 
     def vectors(select):
         both = select[...].astype(F32)
@@ -281,50 +394,49 @@
                 ].astype(BF16)
 
     def send_states(e):
-        to_peers(lambda there: state_out.at[e, there], state_in.at[e], 1 + 4 * e, True)
+        tile_of = lambda there: state_out.at[e, there]
+        to_peers(tile_of, state_in.at[e, frame], 1 + 4 * e, True)
+        to_frames(tile_of, state_in.at[e], 1 + 4 * e, e)
 
         def keep():
-            state_in[e, me] = state_out[e, me]
+            state_in[e, frame, me] = state_out[e, me]
 
         only_owner(keep)
 
     def own(e):
         at = 1 + 4 * e
         back = me >= tiles // 2
+        second = back if e == 0 else jnp.logical_not(back)
+
+        def step(g, i, memory):
+            p = jnp.where(back, peers - 1 - i, i)
+            pair = dec_in[g, p]
+            spent = jnp.where(second, pair[1:2, :], pair[0:1, :])
+            return jnp.exp(spent) * memory + state_in[e, g, p].astype(F32)
+
+        def through(o, memory):
+            g = jnp.where(back, frames - 1 - o, o)
+            if e == 0:
+                all_of(dec_in.at[g], cross_sem.at[2, g])
+            all_of(state_in.at[e, g], cross_sem.at[e, g])
+            for i in range(peers):
+                memory = step(g, i, memory)
+            return memory
+
         if e == 0:
-            arrived(dec_in, 0, peers - 1)
-        arrived(state_in.at[e], at, peers - 1)
-        second = back if e == 0 else jnp.logical_not(back)
-        memory = jnp.zeros((PACK, LANES), F32)
-        total = jnp.zeros((1, LANES), F32)
-        totals = []
+            arrived(dec_in.at[frame], 0, peers - 1)
+        arrived(state_in.at[e, frame], at, peers - 1)
+        memory = lax.fori_loop(
+            0,
+            jnp.where(back, frames - 1 - frame, frame),
+            through,
+            jnp.zeros((PACK, LANES), F32),
+        )
         for i in range(peers):
             p = jnp.where(back, peers - 1 - i, i)
-            pair = dec_in[p]
-            spent = jnp.where(second, pair[1:2, :], pair[0:1, :])
-            inner[i] = memory
-            totals.append(total)
-            memory = jnp.exp(spent) * memory + state_in[e, p].astype(F32)
-            total = total + spent
-        frame_in[e, frame, 0:PACK, :] = memory
-        frame_in[e, frame, PACK : PACK + 8, :] = jnp.broadcast_to(total, (8, LANES))
-
-        def one(o, _):
-            there = lax.rem(frame + o, frames)
-            remote(frame_in.at[e, frame], frame_in.at[e, frame], at + 1, "frame", there).start()
-            return 0
-
-        lax.fori_loop(1, frames, one, 0)
-        arrived(frame_in.at[e], at + 1, frames - 1)
-        carry = jnp.zeros((PACK, LANES), F32)
-        for i in range(frames - 1):
-            g = jnp.where(back, frames - 1 - i, i)
-            reached = jnp.where(back, g > frame, g < frame)
-            new = jnp.exp(frame_in[e, g, PACK : PACK + 1, :]) * carry + frame_in[e, g, 0:PACK, :]
-            carry = jnp.where(reached, new, carry)
-        for i in range(peers):
-            p = jnp.where(back, peers - 1 - i, i)
-            enter_out[e, p] = (inner[i] + jnp.exp(totals[i]) * carry).astype(BF16)
+            enter_out[e, p] = memory.astype(BF16)
+            if i < peers - 1:
+                memory = step(frame, i, memory)
         to_peers(lambda there: enter_out.at[e, there], enter_in.at[e], at + 2, False)
         enter_in[e, me] = enter_out[e, me]
 
@@ -394,11 +506,14 @@
 
     row_values = project(tokens[...], row_gain, row_in)
     stage(0, 0, ends(0, 0, row_values, False))
+    until("col_out")
     col_pulled = mm(cotangent[...], col_out[...], 1, 1).astype(BF16)
     stage(0, 1, ends(1, 1, col_pulled, True))
     send_states(0)
+    until("block")
     local_scan(0, 0, row_values, False)
     local_scan(1, 1, col_pulled, True)
+    until("open_row")
     only_owner(lambda: own(0))
     row_state, col_state = entering(0)
     row_scanned = finish_scan(0, 0, row_state, False)
@@ -431,9 +546,10 @@
             sent(ref, at, peers - 1)
 
     drain(dec_out, 0, True)
+    sent(dec_out, 0, (frames - 1) * (tiles // 2))
     for e in range(2):
         drain(state_out.at[e], 1 + 4 * e, True)
-        only_owner(lambda: sent(frame_in.at[e], 2 + 4 * e, frames - 1))
+        sent(state_out.at[e], 1 + 4 * e, (frames - 1) * (tiles // 2))
         only_owner(lambda: sent(enter_out.at[e], 3 + 4 * e, peers - 1))
         drain(swap_out.at[e], 9 + e, False)
 
@@ -474,27 +590,28 @@
     mixed, grad = pl.pallas_call(
         functools.partial(kernel, (peers, frames, heads, width, parts)),
         out_shape=(out, out),
-        in_specs=[vmem] * len(operands),
+        in_specs=[pl.BlockSpec(memory_space=pltpu.HBM)] * len(operands),
         out_specs=(vmem, vmem),
-        scratch_shapes=[
+        scratch_shapes=[pltpu.VMEM(a.shape, a.dtype) for a in operands]
+        + [
+            pltpu.SemaphoreType.DMA((len(operands),)),
             pltpu.VMEM((2, T, model), F32),
             pltpu.VMEM((2, T, model), F32),
             pltpu.VMEM((2, T, model), F32),
             pltpu.VMEM((strips, 2, LANES), F32),
-            pltpu.VMEM((peers, 2, LANES), F32),
+            pltpu.VMEM((frames, peers, 2, LANES), F32),
             pltpu.VMEM((2, tiles, PACK, LANES), BF16),
-            pltpu.VMEM((2, peers, PACK, LANES), BF16),
-            pltpu.VMEM((peers, PACK, LANES), F32),
-            pltpu.VMEM((2, frames, PACK + 8, LANES), F32),
+            pltpu.VMEM((2, frames, peers, PACK, LANES), BF16),
             pltpu.VMEM((2, peers, PACK, LANES), BF16),
             pltpu.VMEM((2, tiles, PACK, LANES), BF16),
             pltpu.VMEM((2, peers, share, model // parts), BF16),
             pltpu.VMEM((2, peers, share, model // parts), BF16),
             pltpu.SemaphoreType.DMA((11,)),
             pltpu.SemaphoreType.DMA((11,)),
+            pltpu.SemaphoreType.DMA((3, frames)),
         ],
         compiler_params=pltpu.CompilerParams(
-            collective_id=0, has_side_effects=True, vmem_limit_bytes=48 * 1024 * 1024
+            collective_id=0, has_side_effects=True, vmem_limit_bytes=62 * 1024 * 1024
         ),
     )(*operands)
     return (mixed.reshape(cotangent.shape), grad.reshape(tokens.shape))

time: 60.8 us -> 42 us (0.69); the launches traced: 59.9 us -> 41.8 us
  local copies, waits for them, and re-layouts: 18.9 us -> 2.14 us
  Pallas kernels: 40.3 us -> 39 us
    unnamed x48 -> x4, local copies, waits for them, and re-layouts: 18.9 us -> 2.14 us
    pallas_call x1, Pallas kernels: 40.3 us -> 39 us  [body(): pl.pallas_call(functools.partial(kernel, (peers, frames, heads, width, pa...]
where the time goes in v2:
time: 42 us; the launch traced here: 41.8 us
  Pallas kernels  39 us (93%)
  local copies, waits for them, and re-layouts  2.14 us (5%)
  between operations  0.65 us (2%)
    pallas_call x1, Pallas kernels, body(): pl.pallas_call(functools.partial(kernel, (peers, frames, heads, width, pa...  39 us
    unnamed x4, local copies, waits for them, and re-layouts  2.14 us

profile of v2, /device:TPU:0, one launch (start us, length us, event | category | flops | bytes accessed | tf_op | source)
XLA Modules:
  0.0 41.8 jit_solution(12134423856264957917)
XLA Ops:
  0.6 39.0 %shard_map.230 = (bf16[64,512]{1,0:T(8,128)(2,1)}, bf16[64,512]{1,0:T(8,128)(2,1)}) custom-call(bf16[64,512]{1,0:T(8,128)(2,1)} %bitcast.12, bf16[64,64]{1,0:T(8,128)(2,1)} %bitcast.16, f32[8,2,32]{2,1,0:T(2,128)} %bitcast.18, f32[1,512]{1,0:T(1,128)} %bitcast.20, f32[1,8]{1,0:T(1,128)} %bitcast.22, bf16[512,512]{1,0:T(8,128)(2,1)} %refs_5_.1, ...), custom_call_target="tpu_custom_call" | custom-call | tf_op jit(solution)/shard_map/pallas_call | solution.py:590
  39.6 0.0 copy-start
  39.6 1.5 %copy.27 = bf16[1,2,32,512]{3,2,1,0:T(8,128)(2,1)} copy(bf16[1,2,32,512]{3,2,1,0:T(8,128)(2,1)} %bitcast.15) | data formatting | bytes 131072
  41.1 0.0 copy-done
  41.1 0.6 %copy.28 = bf16[1,2,32,512]{3,2,1,0:T(8,128)(2,1)} copy(bf16[1,2,32,512]{3,2,1,0:T(8,128)(2,1)S(1)} %bitcast.14) | data formatting | bytes 131072
Async XLA Ops:
  39.6 1.5 %copy-start = (bf16[64,512]{1,0:T(8,128)(2,1)S(1)}, bf16[64,512]{1,0:T(8,128)(2,1)}, u32[]{:S(2)}) copy-start(bf16[64,512]{1,0:T(8,128)(2,1)} %get-tuple-element.5) | copy-start | bytes 196612

commit v3 on v2

--- a/solution.py
+++ b/solution.py
@@ -235,10 +235,10 @@
     def to_frames(src_of, dst, at, slot):
         def one(o, _):
             there = lax.rem(frame + o, frames)
-            base = jnp.where(there > frame, 0, tiles // 2)
+            base = jnp.where(there > frame, 0, 1)
 
             def owner(i, c):
-                k = base + lax.rem(me + i, tiles // 2)
+                k = base + 2 * lax.rem(me // 2 + i, tiles // 2)
                 pltpu.make_async_remote_copy(
                     src_ref=src_of(k),
                     dst_ref=dst.at[frame, me],
@@ -294,10 +294,10 @@
             dec_out[j, m : m + 1, :] = cum_ref[m, T - 1 : T, j * LANES : (j + 1) * LANES]
 
     pl.semaphore_wait(barrier, peers * frames - 1)
-    strip_of = lambda there: dec_out.at[lax.rem(there, strips)]
+    strip_of = lambda there: dec_out.at[lax.rem(there // 2, strips)]
     to_peers(strip_of, dec_in.at[frame], 0, True)
     to_frames(strip_of, dec_in, 0, 2)
-    dec_in[frame, me] = dec_out[lax.rem(me, strips)]
+    dec_in[frame, me] = dec_out[lax.rem(me // 2, strips)]
 
     until("col_skip")
 
@@ -389,23 +389,52 @@
     def stage(e, a, state):
         for i in range(halves):
             for j in range(strips):
-                state_out[e, (a * halves + i) * strips + j] = state[
+                state_out[e, 2 * (i * strips + j) + a] = state[
                     i * PACK : (i + 1) * PACK, j * LANES : (j + 1) * LANES
                 ].astype(BF16)
 
-    def send_states(e):
-        tile_of = lambda there: state_out.at[e, there]
-        to_peers(tile_of, state_in.at[e, frame], 1 + 4 * e, True)
-        to_frames(tile_of, state_in.at[e], 1 + 4 * e, e)
+    def owns(a):
+        return jnp.logical_and(lax.rem(me, 2) == a, me < tiles)
+
+    def send_states(e, a):
+        count = tiles // 2
+        at = 1 + 4 * e
+
+        def one(i, c):
+            k = a + 2 * lax.rem(me // 2 + 1 + i, count)
+            copy = remote(state_out.at[e, k], state_in.at[e, frame, me], at, "seq", k)
+            pl.when(k != me)(copy.start)
+            return c
+
+        lax.fori_loop(0, count, one, 0)
 
         def keep():
             state_in[e, frame, me] = state_out[e, me]
 
-        only_owner(keep)
+        pl.when(owns(a))(keep)
+
+        def onward(o, _):
+            there = frame + 1 + o if a == 0 else frame - 1 - o
+
+            def owner(i, c):
+                k = a + 2 * lax.rem(me // 2 + i, count)
+                pltpu.make_async_remote_copy(
+                    src_ref=state_out.at[e, k],
+                    dst_ref=state_in.at[e, frame, me],
+                    send_sem=send_sem.at[at],
+                    recv_sem=cross_sem.at[e, frame],
+                    device_id={"seq": k, "frame": there},
+                    device_id_type=pl.DeviceIdType.MESH,
+                ).start()
+                return c
+
+            return lax.fori_loop(0, count, owner, 0)
+
+        lax.fori_loop(0, frames - 1 - frame if a == 0 else frame, onward, 0)
 
     def own(e):
         at = 1 + 4 * e
-        back = me >= tiles // 2
+        back = lax.rem(me, 2) == 1
         second = back if e == 0 else jnp.logical_not(back)
 
         def step(g, i, memory):
@@ -437,26 +466,23 @@
             enter_out[e, p] = memory.astype(BF16)
             if i < peers - 1:
                 memory = step(frame, i, memory)
-        to_peers(lambda there: enter_out.at[e, there], enter_in.at[e], at + 2, False)
+        landing = at + 1 + jnp.where(back, 1, 0)
+        to_peers(lambda there: enter_out.at[e, there], enter_in.at[e], landing, False)
         enter_in[e, me] = enter_out[e, me]
 
-    def entering(e):
-        if tiles < peers:
-            pl.when(me < tiles)(lambda: arrived(enter_in.at[e], 3 + 4 * e, tiles - 1))
-            pl.when(me >= tiles)(lambda: arrived(enter_in.at[e], 3 + 4 * e, tiles))
-        else:
-            arrived(enter_in.at[e], 3 + 4 * e, tiles - 1)
-        return tuple(
-            jnp.concatenate(
-                [
-                    jnp.concatenate(
-                        [enter_in[e, (a * halves + i) * strips + j] for j in range(strips)], axis=1
-                    )
-                    for i in range(halves)
-                ],
-                axis=0,
-            )
-            for a in range(2)
+    def entering(e, a):
+        count = tiles // 2
+        at = 2 + 4 * e + a
+        pl.when(owns(a))(lambda: arrived(enter_in.at[e], at, count - 1))
+        pl.when(jnp.logical_not(owns(a)))(lambda: arrived(enter_in.at[e], at, count))
+        return jnp.concatenate(
+            [
+                jnp.concatenate(
+                    [enter_in[e, 2 * (i * strips + j) + a] for j in range(strips)], axis=1
+                )
+                for i in range(halves)
+            ],
+            axis=0,
         )
 
     def finish_scan(m, slot, state, backward):
@@ -474,8 +500,7 @@
         normed = (floats * factor_of(floats) * gain[...]).astype(BF16)
         return mm(normed, weight[...]).astype(BF16)
 
-    def input_gradient(values, incoming, scanned, gain, weight):
-        returned = mm(scanned, weight[...], 1, 1)
+    def input_gradient(values, incoming, returned, gain):
         floats = values.astype(F32)
         factor = factor_of(floats)
         scaled = gain[...] * returned
@@ -501,42 +526,41 @@
         stacked = mm(pack[...], packed).astype(BF16)
         return jnp.concatenate([stacked[j * T : (j + 1) * T, :] for j in range(parts)], axis=1)
 
-    def ends(m, slot, values, backward):
-        return leaves(m, values, backward)
-
     row_values = project(tokens[...], row_gain, row_in)
-    stage(0, 0, ends(0, 0, row_values, False))
+    stage(0, 0, leaves(0, row_values, False))
+    send_states(0, 0)
     until("col_out")
     col_pulled = mm(cotangent[...], col_out[...], 1, 1).astype(BF16)
-    stage(0, 1, ends(1, 1, col_pulled, True))
-    send_states(0)
+    stage(0, 1, leaves(1, col_pulled, True))
+    send_states(0, 1)
     until("block")
     local_scan(0, 0, row_values, False)
     local_scan(1, 1, col_pulled, True)
     until("open_row")
     only_owner(lambda: own(0))
-    row_state, col_state = entering(0)
-    row_scanned = finish_scan(0, 0, row_state, False)
+    row_scanned = finish_scan(0, 0, entering(0, 0), False)
     row_mixed = (tokens[...].astype(F32) + mm(row_scanned, row_out[...])).astype(BF16)
     swap_send(0, row_mixed, pack_row)
-    col_scanned = finish_scan(1, 1, col_state, True)
+    col_scanned = finish_scan(1, 1, entering(0, 1), True)
+    col_returned = mm(col_scanned, col_in[...], 1, 1)
     col_tokens = swap_take(0, open_col)
-    col_grad = input_gradient(col_tokens, cotangent[...], col_scanned, col_gain, col_in)
+    col_grad = input_gradient(col_tokens, cotangent[...], col_returned, col_gain)
     swap_send(1, col_grad, pack_col)
     col_values = project(col_tokens, col_gain, col_in)
-    stage(1, 0, ends(1, 0, col_values, False))
+    stage(1, 0, leaves(1, col_values, False))
+    send_states(1, 0)
     local_scan(1, 0, col_values, False)
     row_grad = swap_take(1, open_row)
     row_pulled = mm(row_grad, row_out[...], 1, 1).astype(BF16)
-    stage(1, 1, ends(0, 1, row_pulled, True))
-    send_states(1)
+    stage(1, 1, leaves(0, row_pulled, True))
+    send_states(1, 1)
     local_scan(0, 1, row_pulled, True)
     only_owner(lambda: own(1))
-    col_state, row_state = entering(1)
-    col_scanned = finish_scan(1, 0, col_state, False)
+    col_scanned = finish_scan(1, 0, entering(1, 0), False)
     mixed[...] = (col_tokens.astype(F32) + mm(col_scanned, col_out[...])).astype(BF16)
-    row_scanned = finish_scan(0, 1, row_state, True)
-    grad_tokens[...] = input_gradient(tokens[...], row_grad, row_scanned, row_gain, row_in)
+    row_scanned = finish_scan(0, 1, entering(1, 1), True)
+    row_returned = mm(row_scanned, row_in[...], 1, 1)
+    grad_tokens[...] = input_gradient(tokens[...], row_grad, row_returned, row_gain)
 
     def drain(ref, at, owners):
         if owners and tiles < peers:
@@ -550,7 +574,8 @@
     for e in range(2):
         drain(state_out.at[e], 1 + 4 * e, True)
         sent(state_out.at[e], 1 + 4 * e, (frames - 1) * (tiles // 2))
-        only_owner(lambda: sent(enter_out.at[e], 3 + 4 * e, peers - 1))
+        landing = 2 + 4 * e + lax.rem(me, 2)
+        only_owner(lambda: sent(enter_out.at[e], landing, peers - 1))
         drain(swap_out.at[e], 9 + e, False)
 
 

time: 42 us -> 40.5 us (0.964)
  Pallas kernels: 39 us -> 37.5 us
    pallas_call x1, Pallas kernels: 39 us -> 37.5 us  [body(): pl.pallas_call(functools.partial(kernel, (peers, frames, heads, width, pa...]
where the time goes in v3:
time: 40.5 us; the launch traced here: 40.3 us
  Pallas kernels  37.5 us (93%)
  local copies, waits for them, and re-layouts  2.14 us (5%)
  between operations  0.65 us (2%)
    pallas_call x1, Pallas kernels, body(): pl.pallas_call(functools.partial(kernel, (peers, frames, heads, width, pa...  37.5 us
    unnamed x4, local copies, waits for them, and re-layouts  2.14 us

profile of v3, /device:TPU:0, one launch (start us, length us, event | category | flops | bytes accessed | tf_op | source)
XLA Modules:
  0.0 40.3 jit_solution(16589925170441694835)
XLA Ops:
  0.6 37.5 %shard_map.230 = (bf16[64,512]{1,0:T(8,128)(2,1)}, bf16[64,512]{1,0:T(8,128)(2,1)}) custom-call(bf16[64,512]{1,0:T(8,128)(2,1)} %bitcast.12, bf16[64,64]{1,0:T(8,128)(2,1)} %bitcast.16, f32[8,2,32]{2,1,0:T(2,128)} %bitcast.18, f32[1,512]{1,0:T(1,128)} %bitcast.20, f32[1,8]{1,0:T(1,128)} %bitcast.22, bf16[512,512]{1,0:T(8,128)(2,1)} %refs_5_.1, ...), custom_call_target="tpu_custom_call" | custom-call | tf_op jit(solution)/shard_map/pallas_call | solution.py:615
  38.1 0.0 copy-start
  38.1 1.5 %copy.27 = bf16[1,2,32,512]{3,2,1,0:T(8,128)(2,1)} copy(bf16[1,2,32,512]{3,2,1,0:T(8,128)(2,1)} %bitcast.15) | data formatting | bytes 131072
  39.6 0.0 copy-done
  39.6 0.6 %copy.28 = bf16[1,2,32,512]{3,2,1,0:T(8,128)(2,1)} copy(bf16[1,2,32,512]{3,2,1,0:T(8,128)(2,1)S(1)} %bitcast.14) | data formatting | bytes 131072
Async XLA Ops:
  38.1 1.5 %copy-start = (bf16[64,512]{1,0:T(8,128)(2,1)S(1)}, bf16[64,512]{1,0:T(8,128)(2,1)}, u32[]{:S(2)}) copy-start(bf16[64,512]{1,0:T(8,128)(2,1)} %get-tuple-element.5) | copy-start | bytes 196612
